TPU v7x, 128 devices: a whole 4x4x4 slice. The times are simulated.
128 devices in a mesh: batch: 8 (over y, core), seq: 16 (over x, z).
Axes of the slice: x: 4, y: 4, z: 4, core: 2. Of those that a mesh axis runs over, the one named last changes fastest.
Arguments:
- feats: bfloat16 [16, 1024, 512], P('batch', 'seq'), may hold values from -6 to 6
- lengths: int32 [16], P('batch'), may hold values from 256 to 1024, as said below
- skip_flag: int32 [8], P('batch'), may hold values from 0 to 1, as said below
- cotangent: bfloat16 [16, 1024, 768], P('batch', 'seq'), may hold values from -6 to 6
- input_gain: bfloat16 [512], replicated, may hold values from 0.5 to 1.5
- input_shift: bfloat16 [512], replicated, may hold values from -3 to 3
- proj_weight: bfloat16 [512, 768], replicated, may hold values from -0.25 to 0.25
- proj_bias: bfloat16 [768], replicated, may hold values from -3 to 3
- conv_weight: bfloat16 [768, 48, 128], replicated, may hold values from -0.078125 to 0.078125
- conv_bias: bfloat16 [768], replicated, may hold values from -3 to 3
- encoder_gain: bfloat16 [768], replicated, may hold values from 0.5 to 1.5
- encoder_shift: bfloat16 [768], replicated, may hold values from -3 to 3
- qkv_weight: bfloat16 [768, 2304], replicated, may hold values from -0.21875 to 0.21875
- query_bias: bfloat16 [768], replicated, may hold values from -3 to 3
- value_bias: bfloat16 [768], replicated, may hold values from -3 to 3
- output_weight: bfloat16 [768, 768], replicated, may hold values from -3.5 to 3.5
- output_bias: bfloat16 [768], replicated, may hold values from -3 to 3
- middle_gain: bfloat16 [768], replicated, may hold values from 0.5 to 1.5
- middle_shift: bfloat16 [768], replicated, may hold values from -3 to 3
- inner_weight: bfloat16 [768, 3072], replicated, may hold values from -0.21875 to 0.21875
- inner_bias: bfloat16 [3072], replicated, may hold values from -3 to 3
- outer_weight: bfloat16 [3072, 768], replicated, may hold values from -0.109375 to 0.109375
- outer_bias: bfloat16 [768], replicated, may hold values from -3 to 3
- final_gain: bfloat16 [768], replicated, may hold values from 0.5 to 1.5
- final_shift: bfloat16 [768], replicated, may hold values from -3 to 3
Outputs:
- activations: bfloat16 [16, 1024, 768], P('batch', 'seq')
- grad_feats: float32 [16, 1024, 512], P('batch', 'seq')
- grad_input_gain: float32 [512], P(('batch', 'seq'))
- grad_input_shift: float32 [512], P(('batch', 'seq'))
- grad_proj_weight: float32 [512, 768], P(('batch', 'seq'))
- grad_proj_bias: float32 [768], P(('batch', 'seq'))
- grad_conv_weight: float32 [768, 48, 128], P(('batch', 'seq'))
- grad_conv_bias: float32 [768], P(('batch', 'seq'))
- grad_encoder_gain: float32 [768], P(('batch', 'seq'))
- grad_encoder_shift: float32 [768], P(('batch', 'seq'))
- grad_qkv_weight: float32 [768, 2304], P(('batch', 'seq'))
- grad_query_bias: float32 [768], P(('batch', 'seq'))
- grad_value_bias: float32 [768], P(('batch', 'seq'))
- grad_output_weight: float32 [768, 768], P(('batch', 'seq'))
- grad_output_bias: float32 [768], P(('batch', 'seq'))
- grad_middle_gain: float32 [768], P(('batch', 'seq'))
- grad_middle_shift: float32 [768], P(('batch', 'seq'))
- grad_inner_weight: float32 [768, 3072], P(('batch', 'seq'))
- grad_inner_bias: float32 [3072], P(('batch', 'seq'))
- grad_outer_weight: float32 [3072, 768], P(('batch', 'seq'))
- grad_outer_bias: float32 [768], P(('batch', 'seq'))
- grad_final_gain: float32 [768], P(('batch', 'seq'))
- grad_final_shift: float32 [768], P(('batch', 'seq'))
Inputs may be any that keep to these rules, and one draw needn't show every extreme that they name: `lengths`: in each bucket of 2 utterances one, chosen by the seed, has all 1024 frames. `skip_flag`: at least one bucket keeps the feed-forward branch and at least one drops it.
All inputs are finite; a program needn't handle non-finite values.
Results may differ from a plain program's by a relative error of at most 0.0208.
Values may be sent and summed in bfloat16 or wider, within the bound.
No kernel may reach another device: no remote copies, remote signals or barrier semaphores. Data moves between devices by JAX's collectives and lax.ppermute only.
A program may use at most 704 MiB of HBM per device.

v0:
```python
import jax
import jax.numpy as jnp
from jax import lax
from jax.sharding import PartitionSpec as P

HEADS = 12
GROUPS = 16


norm_eps = 1e-05
head_scale = 0.125
neg_fill = -1e30
tap_span = 16


def extended(block, sides, width):
    for axis, dim in sides:
        count = lax.axis_size(axis)
        forward = [(i, i + 1) for i in range(count - 1)]
        backward = [(target, source) for source, target in forward]
        low = lax.ppermute(
            lax.slice_in_dim(block, block.shape[dim] - width, None, axis=dim), axis, forward
        )
        high = lax.ppermute(lax.slice_in_dim(block, 0, width, axis=dim), axis, backward)
        block = jnp.concatenate([low, block, high], axis=dim)
    return block


def layer_norm(values, scale_vec, shift_vec):
    center = values - jnp.mean(values, axis=-1, keepdims=True)
    spread = jnp.mean(center * center, axis=-1, keepdims=True)
    return center * lax.rsqrt(spread + norm_eps) * scale_vec + shift_vec


def norm_back(values, scale_vec, shift_vec, incoming):
    _, pull = jax.vjp(layer_norm, values, scale_vec, shift_vec)
    return pull(incoming)


def gelu_exact(values):
    return jax.nn.gelu(values, approximate=False)


def gelu_back(values, incoming):
    _, pull = jax.vjp(gelu_exact, values)
    return pull(incoming)[0]


def matmul(left, right):
    return jnp.dot(left, right, preferred_element_type=jnp.float32)


def matmul_left_t(left, right):
    return lax.dot_general(
        left, right, (((0,), (0,)), ((), ())), preferred_element_type=jnp.float32
    )


def matmul_right_t(left, right):
    return lax.dot_general(
        left, right, (((1,), (1,)), ((), ())), preferred_element_type=jnp.float32
    )


def tap_window(padded, tap_block, frames):
    utts_here = padded.shape[0]
    model_width = padded.shape[2]
    group_width = model_width // GROUPS
    pieces = [
        padded[:, tap_block * tap_span + position : tap_block * tap_span + position + frames, :]
        for position in range(tap_span)
    ]
    stacked = jnp.stack(pieces, axis=2)
    stacked = stacked.reshape(utts_here, frames, tap_span, GROUPS, group_width).transpose(
        0, 1, 3, 2, 4
    )
    return stacked.reshape(utts_here * frames, GROUPS, tap_span * group_width)


def arrange_kernel(weight):
    model_width, group_width, kernel = weight.shape
    blocks = kernel // tap_span
    grouped = weight.reshape(GROUPS, group_width, group_width, blocks, tap_span)
    return grouped.transpose(3, 0, 4, 2, 1).reshape(
        blocks, GROUPS, tap_span * group_width, group_width
    )


def conv_apply(padded, arranged, frames):
    blocks = arranged.shape[0]
    group_width = arranged.shape[3]
    running = jnp.zeros((padded.shape[0] * frames, GROUPS, group_width), jnp.float32)
    for tap_block in range(blocks):
        window = tap_window(padded, tap_block, frames)
        running = running + jnp.einsum(
            "rgi,gio->rgo", window, arranged[tap_block], preferred_element_type=jnp.float32
        )
    return running.reshape(-1, GROUPS * group_width)


def conv_weight_grad(padded, grad_conv_b, frames, kernel):
    model_width = grad_conv_b.shape[1]
    group_width = model_width // GROUPS
    blocks = kernel // tap_span
    grad_groups = grad_conv_b.reshape(-1, GROUPS, group_width)
    products = []
    for tap_block in range(blocks):
        window = tap_window(padded, tap_block, frames)
        products.append(
            jnp.einsum("rgi,rgo->gio", window, grad_groups, preferred_element_type=jnp.float32)
        )
    stacked = jnp.stack(products, axis=0).reshape(
        blocks, GROUPS, tap_span, group_width, group_width
    )
    return stacked.transpose(1, 4, 3, 0, 2).reshape(model_width, group_width, kernel)


def split_heads(values):
    return values.reshape(values.shape[0], values.shape[1], HEADS, -1)


def masked_scores(query_heads, key_heads, key_live):
    raw = jnp.einsum("uqhd,ukhd->uhqk", query_heads, key_heads, preferred_element_type=jnp.float32)
    return jnp.where(key_live[:, None, None, :], raw * head_scale, neg_fill)


def local(
    feats,
    lengths,
    skip_flag,
    cotangent,
    input_gain,
    input_shift,
    proj_weight,
    proj_bias,
    conv_weight,
    conv_bias,
    encoder_gain,
    encoder_shift,
    qkv_weight,
    query_bias,
    value_bias,
    output_weight,
    output_bias,
    middle_gain,
    middle_shift,
    inner_weight,
    inner_bias,
    outer_weight,
    outer_bias,
    final_gain,
    final_shift,
):
    f32 = jnp.float32
    bf16 = jnp.bfloat16
    utts_here, frames, _ = feats.shape
    row_count = utts_here * frames
    model_width = proj_weight.shape[1]
    kernel = conv_weight.shape[2]
    halo_reach = kernel // 2
    frame_index = lax.axis_index("seq") * frames + jnp.arange(frames, dtype=jnp.int32)
    own_live = frame_index[None, :] < lengths[:, None]
    live_rows = own_live.astype(f32).reshape(row_count, 1)
    keep_scale = (1 - skip_flag[0]).astype(f32)
    in_gain = input_gain.astype(f32)
    in_shift = input_shift.astype(f32)
    enc_gain = encoder_gain.astype(f32)
    enc_shift = encoder_shift.astype(f32)
    mid_gain = middle_gain.astype(f32)
    mid_shift = middle_shift.astype(f32)
    fin_gain = final_gain.astype(f32)
    fin_shift = final_shift.astype(f32)
    group_width = model_width // GROUPS
    forward_kernel = arrange_kernel(conv_weight)
    flipped = jnp.flip(
        conv_weight.reshape(GROUPS, group_width, group_width, kernel).transpose(0, 2, 1, 3), axis=3
    ).reshape(model_width, group_width, kernel)
    backward_kernel = arrange_kernel(flipped)
    inputs = feats.astype(f32).reshape(row_count, -1)
    normed = layer_norm(inputs, in_gain, in_shift)
    normed_b = normed.astype(bf16)
    masked = (matmul(normed_b, proj_weight) + proj_bias.astype(f32)) * live_rows
    masked_b = masked.astype(bf16).reshape(utts_here, frames, model_width)
    padded = extended(masked_b, (("seq", 1),), halo_reach)
    conv_pre = conv_apply(padded, forward_kernel, frames) + conv_bias.astype(f32)
    summed = masked + gelu_exact(conv_pre)
    hidden = layer_norm(summed, enc_gain, enc_shift)
    hidden_b = hidden.astype(bf16)
    qkv_bias = jnp.concatenate(
        [query_bias.astype(f32), jnp.zeros((model_width,), f32), value_bias.astype(f32)]
    )
    qkv_b = (matmul(hidden_b, qkv_weight) + qkv_bias).astype(bf16)
    query_b = qkv_b[:, :model_width].reshape(utts_here, frames, model_width)
    key_b = qkv_b[:, model_width : 2 * model_width].reshape(utts_here, frames, model_width)
    value_b = qkv_b[:, 2 * model_width :].reshape(utts_here, frames, model_width)
    gathered_keys, gathered_values = (
        lax.all_gather(key_b, "seq", axis=1, tiled=True),
        lax.all_gather(value_b, "seq", axis=1, tiled=True),
    )
    all_frames = gathered_keys.shape[1]
    key_live = jnp.arange(all_frames, dtype=jnp.int32)[None, :] < lengths[:, None]
    query_heads = split_heads(query_b)
    scores = masked_scores(query_heads, split_heads(gathered_keys), key_live)
    row_top = jnp.max(scores, axis=-1, keepdims=True)
    expanded = jnp.exp(scores - row_top)
    row_total = jnp.sum(expanded, axis=-1, keepdims=True)
    attn_probs = expanded / row_total
    log_total = row_top + jnp.log(row_total)
    attended_b = (
        jnp.einsum(
            "uhqk,ukhd->uqhd",
            attn_probs.astype(bf16),
            split_heads(gathered_values),
            preferred_element_type=f32,
        )
        .reshape(row_count, model_width)
        .astype(bf16)
    )
    middle_in = hidden + matmul(attended_b, output_weight) + output_bias.astype(f32)
    middle = layer_norm(middle_in, mid_gain, mid_shift)
    middle_b = middle.astype(bf16)
    inner_pre = matmul(middle_b, inner_weight) + inner_bias.astype(f32)
    inner_b = gelu_exact(inner_pre).astype(bf16)
    outer_out = matmul(inner_b, outer_weight) + outer_bias.astype(f32)
    final_in = middle + keep_scale * outer_out
    result = layer_norm(final_in, fin_gain, fin_shift)
    activations = result.astype(bf16).reshape(utts_here, frames, model_width)
    grad_result = cotangent.astype(f32).reshape(row_count, model_width)
    grad_final_in, grad_final_gain, grad_final_shift = norm_back(
        final_in, fin_gain, fin_shift, grad_result
    )
    grad_outer_b = (keep_scale * grad_final_in).astype(bf16)
    grad_outer_weight = matmul_left_t(inner_b, grad_outer_b)
    grad_outer_bias = jnp.sum(grad_outer_b.astype(f32), axis=0)
    grad_inner_b = gelu_back(inner_pre, matmul_right_t(grad_outer_b, outer_weight)).astype(bf16)
    grad_inner_weight = matmul_left_t(middle_b, grad_inner_b)
    grad_inner_bias = jnp.sum(grad_inner_b.astype(f32), axis=0)
    grad_middle = grad_final_in + matmul_right_t(grad_inner_b, inner_weight)
    grad_middle_in, grad_middle_gain, grad_middle_shift = norm_back(
        middle_in, mid_gain, mid_shift, grad_middle
    )
    grad_attn_b = grad_middle_in.astype(bf16)
    grad_output_weight = matmul_left_t(attended_b, grad_attn_b)
    grad_output_bias = jnp.sum(grad_attn_b.astype(f32), axis=0)
    grad_attended_b = (
        matmul_right_t(grad_attn_b, output_weight)
        .astype(bf16)
        .reshape(utts_here, frames, model_width)
    )
    back_keys, back_values = (gathered_keys, gathered_values)
    key_heads = split_heads(back_keys)
    value_heads = split_heads(back_values)
    back_probs = jnp.exp(masked_scores(query_heads, key_heads, key_live) - log_total)
    grad_heads = split_heads(grad_attended_b)
    grad_probs = jnp.einsum("uqhd,ukhd->uhqk", grad_heads, value_heads, preferred_element_type=f32)
    row_delta = jnp.sum(back_probs * grad_probs, axis=-1, keepdims=True)
    grad_scores_b = (head_scale * back_probs * (grad_probs - row_delta)).astype(bf16)
    grad_query = jnp.einsum("uhqk,ukhd->uqhd", grad_scores_b, key_heads, preferred_element_type=f32)
    grad_keys_all = jnp.einsum(
        "uhqk,uqhd->ukhd", grad_scores_b, query_heads, preferred_element_type=f32
    ).reshape(utts_here, all_frames, model_width)
    grad_values_all = jnp.einsum(
        "uhqk,uqhd->ukhd", back_probs.astype(bf16), grad_heads, preferred_element_type=f32
    ).reshape(utts_here, all_frames, model_width)
    grad_keys, grad_values = (
        lax.psum_scatter(
            grad_keys_all.astype(jnp.bfloat16), "seq", scatter_dimension=1, tiled=True
        ).astype(jnp.float32),
        lax.psum_scatter(
            grad_values_all.astype(jnp.bfloat16), "seq", scatter_dimension=1, tiled=True
        ).astype(jnp.float32),
    )
    grad_qkv_b = jnp.concatenate(
        [
            grad_query.reshape(row_count, model_width),
            grad_keys.reshape(row_count, model_width),
            grad_values.reshape(row_count, model_width),
        ],
        axis=1,
    ).astype(bf16)
    grad_qkv_weight = matmul_left_t(hidden_b, grad_qkv_b)
    grad_qkv_sums = jnp.sum(grad_qkv_b.astype(f32), axis=0)
    grad_query_bias = grad_qkv_sums[:model_width]
    grad_value_bias = grad_qkv_sums[2 * model_width :]
    grad_hidden = grad_middle_in + matmul_right_t(grad_qkv_b, qkv_weight)
    grad_summed, grad_encoder_gain, grad_encoder_shift = norm_back(
        summed, enc_gain, enc_shift, grad_hidden
    )
    grad_conv_b = gelu_back(conv_pre, grad_summed).astype(bf16)
    grad_conv_bias = jnp.sum(grad_conv_b.astype(f32), axis=0)
    grad_conv_weight = conv_weight_grad(padded, grad_conv_b, frames, kernel)
    grad_padded = extended(
        grad_conv_b.reshape(utts_here, frames, model_width), (("seq", 1),), halo_reach
    )
    grad_masked = grad_summed + conv_apply(grad_padded[:, 1:, :], backward_kernel, frames)
    grad_proj_b = (grad_masked * live_rows).astype(bf16)
    grad_proj_weight = matmul_left_t(normed_b, grad_proj_b)
    grad_proj_bias = jnp.sum(grad_proj_b.astype(f32), axis=0)
    grad_normed = matmul_right_t(grad_proj_b, proj_weight)
    grad_inputs, grad_input_gain, grad_input_shift = norm_back(
        inputs, in_gain, in_shift, grad_normed
    )
    grad_list = [
        grad_input_gain,
        grad_input_shift,
        grad_proj_weight,
        grad_proj_bias,
        grad_conv_weight,
        grad_conv_bias,
        grad_encoder_gain,
        grad_encoder_shift,
        grad_qkv_weight,
        grad_query_bias,
        grad_value_bias,
        grad_output_weight,
        grad_output_bias,
        grad_middle_gain,
        grad_middle_shift,
        grad_inner_weight,
        grad_inner_bias,
        grad_outer_weight,
        grad_outer_bias,
        grad_final_gain,
        grad_final_shift,
    ]
    device_count = lax.axis_size("batch") * lax.axis_size("seq")
    packed = jnp.concatenate(
        [grad_item.reshape(device_count, -1) for grad_item in grad_list], axis=1
    )
    own_grads = lax.psum_scatter(packed, ("batch", "seq"), scatter_dimension=0, tiled=True)
    own_flat = own_grads.reshape(-1)
    outputs = []
    start_col = 0
    for grad_item in grad_list:
        piece_size = grad_item.size // device_count
        piece_shape = (grad_item.shape[0] // device_count,) + grad_item.shape[1:]
        outputs.append(own_flat[start_col : start_col + piece_size].reshape(piece_shape))
        start_col = start_col + piece_size
    return (
        activations,
        grad_inputs.reshape(utts_here, frames, -1),
        outputs[0],
        outputs[1],
        outputs[2],
        outputs[3],
        outputs[4],
        outputs[5],
        outputs[6],
        outputs[7],
        outputs[8],
        outputs[9],
        outputs[10],
        outputs[11],
        outputs[12],
        outputs[13],
        outputs[14],
        outputs[15],
        outputs[16],
        outputs[17],
        outputs[18],
        outputs[19],
        outputs[20],
    )


def solution(mesh):
    placed = (
        P("batch", "seq", None),
        P("batch"),
        P("batch"),
        P("batch", "seq", None),
        P(),
        P(),
        P(),
        P(),
        P(),
        P(),
        P(),
        P(),
        P(),
        P(),
        P(),
        P(),
        P(),
        P(),
        P(),
        P(),
        P(),
        P(),
        P(),
        P(),
        P(),
    )
    return jax.shard_map(
        local,
        mesh=mesh,
        in_specs=placed,
        out_specs=(
            P("batch", "seq", None),
            P("batch", "seq", None),
            P(("batch", "seq")),
            P(("batch", "seq")),
            P(("batch", "seq"), None),
            P(("batch", "seq")),
            P(("batch", "seq"), None, None),
            P(("batch", "seq")),
            P(("batch", "seq")),
            P(("batch", "seq")),
            P(("batch", "seq"), None),
            P(("batch", "seq")),
            P(("batch", "seq")),
            P(("batch", "seq"), None),
            P(("batch", "seq")),
            P(("batch", "seq")),
            P(("batch", "seq")),
            P(("batch", "seq"), None),
            P(("batch", "seq")),
            P(("batch", "seq"), None),
            P(("batch", "seq")),
            P(("batch", "seq")),
            P(("batch", "seq")),
        ),
        check_vma=False,
    )
```

profile of v0, /device:TPU:1, one launch (start us, length us, event | category | flops | bytes accessed | tf_op | source)
XLA Modules:
  0.0 3167.9 jit_solution(17223171683780691567)
XLA Ops:
  26.8 13.1 copy.478
  39.9 35.2 %reshape.1089 = bf16[16,48,48,8,16]{1,0,4,3,2:T(8,128)(2,1)} reshape(bf16[768,48,128]{0,2,1:T(8,128)(2,1)} %copy.478) | data formatting | bytes 18874368 | tf_op jit(solution)/shard_map/reshape | solution.py:83
  75.1 19.1 fusion.301
  152.7 19.5 squeeze.53
  284.3 22.6 copy.481
  382.3 22.6 copy.477
  483.6 22.6 copy.484
  581.5 22.6 copy.487
  763.3 22.5 copy.509
  865.3 22.5 copy.512
  963.4 22.5 copy.515
  1032.1 36.9 %all-gather.5.cloned.1.call-done = bf16[2,1024,768]{2,1,0:T(8,128)(2,1)} async-done(((bf16[2,64,768]{2,1,0:T(8,128)(2,1)}), bf16[2,1024,768]{2,1,0:T(8,128)(2,1)}) %all-gather.5.cloned.1.call-update) | async-done | bytes 3145744 | tf_op jit(solution)/shard_map/all_gather | solution.py:197
  1082.4 35.8 %all-gather.3.cloned.1.call-done = bf16[2,1024,768]{2,1,0:T(8,128)(2,1)} async-done(((bf16[2,64,768]{2,1,0:T(8,128)(2,1)}), bf16[2,1024,768]{2,1,0:T(8,128)(2,1)}) %all-gather.3.cloned.1.call-update) | async-done | bytes 3145744 | tf_op jit(solution)/shard_map/all_gather | solution.py:198
  1187.4 30.0 rev.4
  1217.4 23.2 copy.534
  1240.6 22.5 fusion.300
  1464.2 129.5 %copy.570 = f32[16,48,48,8,16]{4,3,2,1,0:T(8,128)} copy(f32[16,48,48,8,16]{1,2,4,0,3:T(8,128)} %bitcast.324) | data formatting | bytes 37748736 | tf_op jit(solution)/shard_map/transpose | solution.py:115
  1593.7 208.7 %reshape_reshape.15 = f32[128,36864]{1,0:T(8,128)} reshape(f32[16,48,48,8,16]{4,3,2,1,0:T(8,128)} %copy.570) | data formatting | bytes 37748736 | tf_op jit(solution)/shard_map/reshape;reshape | solution.py:328
  1860.6 22.6 copy.550
  1952.9 22.6 copy.548
  2046.6 22.6 copy.546
  2139.6 22.6 copy.544
  2251.1 22.6 copy.542
  2345.5 22.6 copy.538
  2440.0 22.9 copy.536
  2533.0 22.6 copy.533
  2601.4 56.3 %dynamic-update-slice.4 = f32[128,95336]{1,0:T(8,128)} dynamic-update-slice(f32[128,95336]{1,0:T(8,128)} %dynamic-update-slice.3, f32[128,36864]{1,0:T(8,128)} %reshape_reshape.15, s32[]{} %constant.40, s32[]{} %constant.153) | dynamic-update-slice | bytes 37748740
  2663.0 23.2 dynamic-update-slice.8
  2689.7 11.6 dynamic-update-slice.11
  2706.4 33.9 %dynamic-update-slice.15 = f32[128,95336]{1,0:T(8,128)} dynamic-update-slice(f32[128,95336]{1,0:T(8,128)} %dynamic-update-slice.14, f32[128,18432]{1,0:T(8,128)} %reshape.1132, s32[]{} %constant.40, s32[]{} %constant.164) | dynamic-update-slice | bytes 18874372
  2742.0 32.8 %dynamic-update-slice.17 = f32[128,95336]{1,0:T(8,128)} dynamic-update-slice(f32[128,95336]{1,0:T(8,128)} %dynamic-update-slice.16, f32[128,18432]{1,0:T(8,128)} %reshape.1134, s32[]{} %constant.40, s32[]{} %constant.166) | dynamic-update-slice | bytes 18874372
  2782.5 358.9 %all-reduce.3.cloned.1.call-done = f32[128,95336]{1,0:T(8,128)} async-done(((f32[128,95336]{1,0:T(8,128)}), f32[128,95336]{1,0:T(8,128)}) %all-reduce.3.cloned.1.call-update) | async-done | bytes 48812048
  (1268 shorter events, 1722.1 us)
Async XLA Ops:
  7.2 1008.6 %copy-start = (bf16[768,2304]{1,0:T(8,128)(2,1)S(1)}, bf16[768,2304]{1,0:T(8,128)(2,1)}, u32[]{:S(2)}) copy-start(bf16[768,2304]{1,0:T(8,128)(2,1)} %param.37) | copy-start | bytes 10616836
  7.2 1061.8 %all-gather.5.cloned.1.call-start = ((), (), s32[]{:S(2)}) async-start(), calls=%async_computation.3 | async-start | bytes 3342336 | tf_op jit(solution)/shard_map/all_gather | solution.py:197
  9.6 30.3 copy-start.200
  18.7 194.9 %collective-permute-start = (bf16[2,64,768]{2,1,0:T(8,128)(2,1)}, bf16[2,64,768]{2,1,0:T(8,128)(2,1)}, u32[]{:S(2)}, u32[]{:S(2)}) collective-permute-start(bf16[2,64,768]{2,1,0:T(8,128)(2,1)} %bitcast.1), channel_id=1, source_target_pairs={{0,1},{1,2},{2,3},{3,4},{4,5},{5,6},{6,7},{7,8},{8,9},{9,10},{10,1... | collective-permute-start | bytes 589832 | tf_op jit(solution)/shard_map/ppermute | solution.py:21
  23.8 591.7 %collective-permute-start.1 = (bf16[2,64,768]{2,1,0:T(8,128)(2,1)}, bf16[2,64,768]{2,1,0:T(8,128)(2,1)}, u32[]{:S(2)}, u32[]{:S(2)}) collective-permute-start(bf16[2,64,768]{2,1,0:T(8,128)(2,1)} %bitcast.1), channel_id=1, source_target_pairs={{1,0},{2,1},{3,2},{4,3},{5,4},{6,5},{7,6},{8,7},{9,8},{10,9},{11,1... | collective-permute-start | bytes 589832 | tf_op jit(solution)/shard_map/ppermute | solution.py:24
  209.5 802.7 %copy-start.184 = (f32[768]{0:T(1024)}, f32[768]{0:T(1024)S(1)}, u32[]{:S(2)}) copy-start(f32[768]{0:T(1024)S(1)} %convert_element_type.171) | copy-start | bytes 9220
  1018.0 100.1 %all-gather.3.cloned.1.call-start = ((), (), s32[]{:S(2)}) async-start(), calls=%async_computation.2 | async-start | bytes 3342336 | tf_op jit(solution)/shard_map/all_gather | solution.py:198
  1018.8 345.4 %reduce-scatter.3.cloned.1.call-start = ((), (), s32[]{:S(2)}) async-start(), calls=%async_computation.4 | async-start | bytes 3342336 | tf_op jit(solution)/shard_map/reduce_scatter | solution.py:266
  1176.8 189.1 %reduce-scatter.5.cloned.1.call-start = ((), (), s32[]{:S(2)}) async-start(), calls=%async_computation.5 | async-start | bytes 3342336 | tf_op jit(solution)/shard_map/reduce_scatter | solution.py:269
  1187.3 1954.1 %all-reduce.3.cloned.1.call-start = ((), (), s32[]{:S(2)}) async-start(), calls=%async_computation.6 | async-start | bytes 97648640
  1411.7 393.8 %collective-permute-start.3 = (bf16[2,64,768]{2,1,0:T(8,128)(2,1)}, bf16[2,64,768]{2,1,0:T(8,128)(2,1)S(1)}, u32[]{:S(2)}, u32[]{:S(2)}) collective-permute-start(bf16[2,64,768]{2,1,0:T(8,128)(2,1)} %bitcast.43), channel_id=1, source_target_pairs={{1,0},{2,1},{3,2},{4,3},{5,4},{6,5},{7,6},{8,7},{9,8},{10,9},{11,1... | collective-permute-start | bytes 589832 | tf_op jit(solution)/shard_map/ppermute | solution.py:24
  1412.9 760.4 %collective-permute-start.2 = (bf16[2,64,768]{2,1,0:T(8,128)(2,1)}, bf16[2,64,768]{2,1,0:T(8,128)(2,1)}, u32[]{:S(2)}, u32[]{:S(2)}) collective-permute-start(bf16[2,64,768]{2,1,0:T(8,128)(2,1)} %bitcast.43), channel_id=1, source_target_pairs={{0,1},{1,2},{2,3},{3,4},{4,5},{5,6},{6,7},{7,8},{8,9},{9,10},{10,1... | collective-permute-start | bytes 589832 | tf_op jit(solution)/shard_map/ppermute | solution.py:21
  1593.7 208.7 %copy-start.193 = (f32[768]{0:T(1024)S(1)}, f32[768]{0:T(1024)}, u32[]{:S(2)}) copy-start(f32[768]{0:T(1024)} %get-tuple-element.43) | copy-start | bytes 9220
  1593.7 209.4 %copy-start.205 = (f32[768]{0:T(1024)S(1)}, f32[768]{0:T(1024)}, u32[]{:S(2)}) copy-start(f32[768]{0:T(1024)} %get-tuple-element.27) | copy-start | bytes 9220
  1593.7 210.2 %copy-start.204 = (f32[768]{0:T(1024)S(1)}, f32[768]{0:T(1024)}, u32[]{:S(2)}) copy-start(f32[768]{0:T(1024)} %get-tuple-element.34) | copy-start | bytes 9220
  1883.2 47.1 %copy-start.165 = (bf16[2,64,768]{2,1,0:T(8,128)(2,1)S(1)}, bf16[2,64,768]{2,1,0:T(8,128)(2,1)}, u32[]{:S(2)}) copy-start(bf16[2,64,768]{2,1,0:T(8,128)(2,1)} %get-tuple-element.145) | copy-start | bytes 589828
  1975.5 48.5 %copy-start.164 = (bf16[2,64,768]{2,1,0:T(8,128)(2,1)S(1)}, bf16[2,64,768]{2,1,0:T(8,128)(2,1)}, u32[]{:S(2)}) copy-start(bf16[2,64,768]{2,1,0:T(8,128)(2,1)} %get-tuple-element.127) | copy-start | bytes 589828
  2069.1 46.5 %copy-start.163 = (bf16[2,64,768]{2,1,0:T(8,128)(2,1)S(1)}, bf16[2,64,768]{2,1,0:T(8,128)(2,1)}, u32[]{:S(2)}) copy-start(bf16[2,64,768]{2,1,0:T(8,128)(2,1)} %get-tuple-element.108) | copy-start | bytes 589828
  2583.3 74.4 %copy-start.45 = (f32[128,512]{1,0:T(8,128)}, f32[128,512]{1,0:T(8,128)S(1)}, u32[]{:S(2)}) copy-start(f32[128,512]{1,0:T(8,128)S(1)} %get-tuple-element.359) | copy-start | bytes 786436
  2601.4 56.3 %copy-start.178 = (f32[128,6]{1,0:T(8,128)S(1)}, f32[128,6]{1,0:T(8,128)}, u32[]{:S(2)}) copy-start(f32[128,6]{1,0:T(8,128)} %reshape.1124) | copy-start | bytes 9220
  2601.4 58.2 %copy-start.176 = (f32[128,6]{1,0:T(8,128)S(1)}, f32[128,6]{1,0:T(8,128)}, u32[]{:S(2)}) copy-start(f32[128,6]{1,0:T(8,128)} %reshape.1125) | copy-start | bytes 9220
  2601.4 59.9 %copy-start.177 = (f32[128,6]{1,0:T(8,128)S(1)}, f32[128,6]{1,0:T(8,128)}, u32[]{:S(2)}) copy-start(f32[128,6]{1,0:T(8,128)} %reshape.1126) | copy-start | bytes 9220
  2657.7 30.3 copy-start.175
  2657.7 32.0 %copy-start.25 = (f32[128,4608]{1,0:T(8,128)S(1)}, f32[128,4608]{1,0:T(8,128)}, u32[]{:S(2)}) copy-start(f32[128,4608]{1,0:T(8,128)} %reshape.1128) | copy-start | bytes 7077892
  2663.0 38.3 %copy-start.173 = (f32[128,6]{1,0:T(8,128)S(1)}, f32[128,6]{1,0:T(8,128)}, u32[]{:S(2)}) copy-start(f32[128,6]{1,0:T(8,128)} %reshape.1129) | copy-start | bytes 9220
  2663.0 40.0 %copy-start.171 = (f32[128,6]{1,0:T(8,128)S(1)}, f32[128,6]{1,0:T(8,128)}, u32[]{:S(2)}) copy-start(f32[128,6]{1,0:T(8,128)} %reshape.1130) | copy-start | bytes 9220
  2663.0 41.7 %copy-start.172 = (f32[128,6]{1,0:T(8,128)S(1)}, f32[128,6]{1,0:T(8,128)}, u32[]{:S(2)}) copy-start(f32[128,6]{1,0:T(8,128)} %reshape.1131) | copy-start | bytes 9220
  2706.4 33.9 %copy-start.168 = (f32[128,24]{1,0:T(8,128)S(1)}, f32[128,24]{1,0:T(8,128)}, u32[]{:S(2)}) copy-start(f32[128,24]{1,0:T(8,128)} %reshape.1133) | copy-start | bytes 36868
  2742.0 32.8 %copy-start.169 = (f32[128,6]{1,0:T(8,128)S(1)}, f32[128,6]{1,0:T(8,128)}, u32[]{:S(2)}) copy-start(f32[128,6]{1,0:T(8,128)} %reshape.1135) | copy-start | bytes 9220
  2742.0 34.4 %copy-start.170 = (f32[128,6]{1,0:T(8,128)S(1)}, f32[128,6]{1,0:T(8,128)}, u32[]{:S(2)}) copy-start(f32[128,6]{1,0:T(8,128)} %reshape.1136) | copy-start | bytes 9220
  2742.0 36.0 %copy-start.167 = (f32[128,6]{1,0:T(8,128)S(1)}, f32[128,6]{1,0:T(8,128)}, u32[]{:S(2)}) copy-start(f32[128,6]{1,0:T(8,128)} %reshape.1137) | copy-start | bytes 9220
  2779.6 381.5 %copy-start.1 = (bf16[768,2304]{1,0:T(8,128)(2,1)S(1)}, bf16[768,2304]{1,0:T(8,128)(2,1)}, u32[]{:S(2)}) copy-start(bf16[768,2304]{1,0:T(8,128)(2,1)} %param.37) | copy-start | bytes 10616836
  (214 other events, 2643.5 us)
Sparse Core Ops, SparseCore 0:
  1018.1 50.8 all-gather.4
  1071.2 46.8 all-gather.2
  1176.9 73.3 reduce-scatter.2
  1253.5 75.0 reduce-scatter.4
  2779.8 361.6 all-reduce.2
where the time goes:
time: 3220 us; the launch traced here: 3170 us
  local copies, waits for them, and re-layouts  2450 us (76%)
  waiting for transfers between devices  432 us (13%)
  other arithmetic  133 us (4%)
  matrix products  128 us (4%)
    unnamed x742, local copies, waits for them, and re-layouts  598 us
    another operation x272, local copies, waits for them, and re-layouts, tap_window(): stacked = jnp.stack(pieces, axis=2)  581 us
    unnamed x6, waiting for transfers between devices  360 us
    transpose x16, local copies, waits for them, and re-layouts, tap_window(): stacked.reshape(utts_here, frames, tap_span, GROUPS, group_width)  346 us
    another operation x1, local copies, waits for them, and re-layouts, local(): grad_item.reshape(device_count, -1)  209 us
    reshape x16, local copies, waits for them, and re-layouts, tap_window(): return stacked.reshape(utts_here * frames, GROUPS, tap_span * group_width)  178 us
    transpose x1, local copies, waits for them, and re-layouts, conv_weight_grad(): stacked.transpose(1, 4, 3, 0, 2).reshape(model_width, group_width, kernel)  130 us
    squeeze x16, local copies, waits for them, and re-layouts, conv_apply(): arranged[tap_block]  103 us
  transfers between devices with their start and end apart: 9, of which 3 were waited for; matrix products, arithmetic and copies ran while one was open for 49% of the time, Pallas kernels for 0%

commit v1 on v0

v1 whole, which is shorter than its diff:
```python
import functools

import jax
import jax.numpy as jnp
from jax import lax
from jax.experimental import pallas as pl
from jax.experimental.pallas import tpu as pltpu
from jax.sharding import PartitionSpec as P

f32 = jnp.float32
bf16 = jnp.bfloat16
i32 = jnp.int32

norm_eps = 1e-05
head_scale = 0.125
neg_fill = -1e30

D = 768
C_IN = 512
FF = 3072
GROUPS = 16
GW = 48
KW = 128
SUPER = 16
TAP_BLOCKS = 9
ROWS = 128
SEQ = 16
PAIRS = 6
VMEM = 60 * 1024 * 1024
TRANSPOSE_SCRATCH = pltpu.VMEM((D, 128), f32)

(
    R_IN_G, R_IN_S, R_PROJ_B, R_CONV_B, R_ENC_G, R_ENC_S, R_Q_B, R_V_B, R_OUT_B, R_MID_G, R_MID_S, R_INNER_B,
    _r12, _r13, _r14, R_OUTER_B, R_FIN_G, R_FIN_S,
) = range(18)


def nn(a, b):
    return lax.dot_general(a, b, (((1,), (0,)), ((), ())), preferred_element_type=f32)


def nt(a, b):
    return lax.dot_general(a, b, (((1,), (1,)), ((), ())), preferred_element_type=f32)


def tn(a, b):
    return lax.dot_general(a, b, (((0,), (0,)), ((), ())), preferred_element_type=f32)


def iota(shape, dim):
    return lax.broadcasted_iota(i32, shape, dim)


def int_div(x, c):
    return ((x.astype(f32) + 0.5) * (1.0 / c)).astype(i32)


def stats(x):
    c = x - jnp.mean(x, axis=-1, keepdims=True)
    r = lax.rsqrt(jnp.mean(c * c, axis=-1, keepdims=True) + norm_eps)
    return c * r, r


def norm_back(xhat, r, gain, g):
    e = g * gain
    dx = r * (e - jnp.mean(e, axis=-1, keepdims=True) - xhat * jnp.mean(e * xhat, axis=-1, keepdims=True))
    return dx, jnp.sum(g * xhat, axis=0, keepdims=True), jnp.sum(g, axis=0, keepdims=True)


def cdf(x):
    return 0.5 * (1.0 + lax.erf(x * 0.7071067811865476))


def gelu(x):
    return x * cdf(x)


def gelu_slope(x):
    return cdf(x) + x * (0.3989422804014327 * jnp.exp(-0.5 * x * x))


def col_sum(x):
    return jnp.sum(x.astype(f32), axis=0, keepdims=True)


def vec(vecs_ref, row, width=D):
    return vecs_ref[row : row + 1, :width]


def swap_blocks(xs):
    ys = [pltpu.roll(x, f * GW, 1) if f else x for f, x in enumerate(xs)]
    lane = iota((8, 128), 1)
    outs = []
    for g in range(GROUPS):
        tiles = []
        for v in range(D // 128):
            lo, hi = (128 * v) // GW, (128 * v + 127) // GW
            tile = ys[(lo - g) % 16][:, v * 128 : (v + 1) * 128]
            for q in range(lo + 1, hi + 1):
                tile = jnp.where(lane >= q * GW - 128 * v, ys[(q - g) % 16][:, v * 128 : (v + 1) * 128], tile)
            tiles.append(tile)
        w = jnp.concatenate(tiles, axis=1)
        outs.append(pltpu.roll(w, D - g * GW, 1) if g else w)
    return outs


LANE_TILES = D // 128


def rows_to_groups(x, scratch, out_ref):
    for v in range(LANE_TILES):
        scratch[v * ROWS : (v + 1) * ROWS, :] = x[:, v * 128 : (v + 1) * 128]
    outs = swap_blocks(
        [
            jnp.concatenate([scratch[pl.ds(v * ROWS + f, 8, stride=SUPER), :] for v in range(LANE_TILES)], axis=1)
            for f in range(SUPER)
        ]
    )
    for g in range(0, GROUPS, 2):
        out_ref[g * 8 : g * 8 + 16, :] = jnp.concatenate(outs[g : g + 2], axis=0).astype(out_ref.dtype)


def groups_to_rows(in_ref, scratch):
    xs = []
    for g in range(0, GROUPS, 2):
        both = in_ref[g * 8 : g * 8 + 16, :].astype(f32)
        xs += [both[:8], both[8:]]
    for f, x in enumerate(swap_blocks(xs)):
        for v in range(LANE_TILES):
            scratch[pl.ds(v * ROWS + f, 8, stride=SUPER), :] = x[:, v * 128 : (v + 1) * 128]
    return jnp.concatenate([scratch[v * ROWS : (v + 1) * ROWS, :] for v in range(LANE_TILES)], axis=1)


def call(body, out_shapes, *args, scratch=(), smem=(), grid=None, in_specs=None, out_specs=None, flops=0, name=None):
    specs = [
        pl.BlockSpec(memory_space=pltpu.SMEM) if i in smem else pl.BlockSpec(memory_space=pltpu.VMEM)
        for i in range(len(args))
    ]
    bytes_accessed = sum(a.size * a.dtype.itemsize for a in args) + sum(
        s.size * s.dtype.itemsize for s in out_shapes
    )
    kwargs = dict(grid=grid) if grid else {}
    return pl.pallas_call(
        body,
        out_shape=out_shapes,
        in_specs=in_specs or specs,
        out_specs=out_specs or [pl.BlockSpec(memory_space=pltpu.VMEM)] * len(out_shapes),
        scratch_shapes=list(scratch),
        compiler_params=pltpu.CompilerParams(vmem_limit_bytes=VMEM),
        cost_estimate=pl.CostEstimate(flops=flops, bytes_accessed=bytes_accessed, transcendentals=0),
        name=name,
        **kwargs,
    )(*args)


def shape(dims, dtype):
    return jax.ShapeDtypeStruct(dims, dtype)


def live_rows(info):
    row = iota((ROWS, 1), 0)
    frame = (row & 63) + info[2] * 64
    length = jnp.where(row < 64, info[0], info[1])
    return (frame < length).astype(f32)


def project_kernel(info, feats, vecs, weight, normed_out, masked_out, send_out, scratch):
    xhat, _ = stats(feats[...].astype(f32))
    normed = (xhat * vec(vecs, R_IN_G, C_IN) + vec(vecs, R_IN_S, C_IN)).astype(bf16)
    normed_out[...] = normed
    masked = (nn(normed, weight[...]) + vec(vecs, R_PROJ_B)) * live_rows(info)
    masked_out[...] = masked
    rows_to_groups(masked, scratch, send_out)


def toeplitz_kernel(taps, out):
    flat = jnp.concatenate([taps[...].astype(f32), jnp.zeros((GW, D), f32)], axis=1)
    for f in range(SUPER):
        rolled = pltpu.roll(flat, f * GW, 1) if f else flat
        out[f * GW : (f + 1) * GW, :] = rolled.astype(bf16)


def shift_matrix(delta):
    r, c = iota((ROWS, ROWS), 0), iota((ROWS, ROWS), 1)
    frame_r = (r >> 3) * 4 + (r & 3)
    frame_c = (c >> 3) * 4 + (c & 3)
    return ((frame_c == frame_r + delta) & ((r & 4) == (c & 4))).astype(f32).astype(bf16)


def conv_kernel(x, w, out, acc):
    i = pl.program_id(0)

    @pl.when(i == 0)
    def _():
        acc[...] = jnp.zeros_like(acc)

    acc[...] += nt(nn(shift_matrix(i - 4), x[...]).astype(bf16), w[...])

    @pl.when(i == TAP_BLOCKS - 1)
    def _():
        out[...] = acc[...].astype(out.dtype)


def conv_back_kernel(g, w, out, acc):
    i = pl.program_id(0)

    @pl.when(i == 0)
    def _():
        acc[...] = jnp.zeros_like(acc)

    acc[...] += nn(nn(shift_matrix(4 - i), g[...]).astype(bf16), w[...])

    @pl.when(i == TAP_BLOCKS - 1)
    def _():
        out[...] = acc[...].astype(out.dtype)


def conv_weight_kernel(g, x, out, acc, spread):
    i = pl.program_id(0)

    @pl.when(i == 0)
    def _():
        acc[...] = jnp.zeros_like(acc)

    window = nn(shift_matrix(i - 4), x[...]).astype(bf16)
    product = tn(g[...], window)
    lane = iota((GW, D), 1)
    same = product[:GW]
    before = jnp.zeros((GW, D), f32)
    for f in range(1, SUPER):
        rolled = pltpu.roll(product[f * GW : (f + 1) * GW], D - f * GW, 1)
        keep = lane < D - f * GW
        same += jnp.where(keep, rolled, 0.0)
        before += jnp.where(keep, 0.0, rolled)
    acc[i] += same

    @pl.when(i > 0)
    def _():
        acc[i - 1] += before

    @pl.when(i == TAP_BLOCKS - 1)
    def _():
        for v in range(LANE_TILES):
            for j in range(TAP_BLOCKS - 1):
                spread[pl.ds(j, GW, stride=TAP_BLOCKS - 1), :] = acc[j, :, v * 128 : (v + 1) * 128]
            out[:, v * 128 : (v + 1) * 128] = spread[...]


def qkv_kernel(conv, masked, vecs, weight, pre_out, hidden_out, send_out, scratch):
    pre = groups_to_rows(conv, scratch) + vec(vecs, R_CONV_B)
    pre_out[...] = pre
    xhat, _ = stats(masked[...] + gelu(pre))
    hidden = xhat * vec(vecs, R_ENC_G) + vec(vecs, R_ENC_S)
    hidden_out[...] = hidden
    hidden_b = hidden.astype(bf16)
    zero = jnp.zeros((1, D), f32)
    for slot, (block, bias) in enumerate(((1, zero), (2, vec(vecs, R_V_B)), (0, vec(vecs, R_Q_B)))):
        part = (nn(hidden_b, weight[:, block * D : (block + 1) * D]) + bias).astype(bf16)
        for u in range(2):
            for pair in range(PAIRS):
                send_out[u * PAIRS + pair, slot * 64 : (slot + 1) * 64, :] = part[
                    u * 64 : (u + 1) * 64, pair * 128 : (pair + 1) * 128
                ]
    send_out[2 * PAIRS :] = jnp.zeros((SEQ - 2 * PAIRS, 192, 128), bf16)


Q_BLOCK = 256


def attend_kernel(info, qkv, out, log_out):
    keys = qkv[:, 0:64, :].reshape(1024, 128)
    values = qkv[:, 64:128, :].reshape(1024, 128)
    left = iota((Q_BLOCK, 128), 1) < 64
    key_live = iota((Q_BLOCK, 1024), 1) < info[5]
    per = Q_BLOCK // 64

    def step(n, carry):
        query = qkv[pl.ds(n * per, per), 128:192, :].reshape(Q_BLOCK, 128)
        parts, logs = [], []
        for head in range(2):
            own = left if head == 0 else ~left
            scores = nt(jnp.where(own, query, jnp.zeros_like(query)), keys)
            scores = jnp.where(key_live, scores * head_scale, neg_fill)
            top = jnp.max(scores, axis=-1, keepdims=True)
            e = jnp.exp(scores - top)
            total = jnp.sum(e, axis=-1, keepdims=True)
            probs = (e * (1.0 / total)).astype(bf16)
            parts.append(nn(probs, values))
            logs.append(top + jnp.log(total))
        rows = pl.ds(pl.multiple_of(n * Q_BLOCK, Q_BLOCK), Q_BLOCK)
        out[rows, :] = jnp.where(left, parts[0], parts[1]).astype(bf16)
        log_out[rows, :] = jnp.where(left, logs[0], logs[1])
        return carry

    lax.fori_loop(0, 1024 // Q_BLOCK, step, 0)


def attend_back_kernel(info, qkv, grad, logs, out, dk, dv):
    keys = qkv[:, 0:64, :].reshape(1024, 128)
    values = qkv[:, 64:128, :].reshape(1024, 128)
    left = iota((Q_BLOCK, 128), 1) < 64
    key_live = iota((Q_BLOCK, 1024), 1) < info[5]
    per = Q_BLOCK // 64
    dk[...] = jnp.zeros_like(dk)
    dv[...] = jnp.zeros_like(dv)

    def step(n, carry):
        query = qkv[pl.ds(n * per, per), 128:192, :].reshape(Q_BLOCK, 128)
        rows = pl.ds(pl.multiple_of(n * Q_BLOCK, Q_BLOCK), Q_BLOCK)
        go = grad[rows, :]
        parts = []
        for head in range(2):
            own = left if head == 0 else ~left
            q_h = jnp.where(own, query, jnp.zeros_like(query))
            g_h = jnp.where(own, go, jnp.zeros_like(go))
            scores = jnp.where(key_live, nt(q_h, keys) * head_scale, neg_fill)
            probs = jnp.exp(scores - logs[rows, head * 64 : head * 64 + 1])
            grad_probs = nt(g_h, values)
            delta = jnp.sum(probs * grad_probs, axis=-1, keepdims=True)
            grad_scores = (head_scale * probs * (grad_probs - delta)).astype(bf16)
            parts.append(nn(grad_scores, keys))
            dk[...] += tn(grad_scores, q_h)
            dv[...] += tn(probs.astype(bf16), g_h)
        grad_query = jnp.where(left, parts[0], parts[1]).astype(bf16)
        out[pl.ds(n * per, per), 0:64, :] = grad_query.reshape(per, 64, 128)
        return carry

    lax.fori_loop(0, 1024 // Q_BLOCK, step, 0)
    out[:, 64:128, :] = dk[...].astype(bf16).reshape(SEQ, 64, 128)
    out[:, 128:192, :] = dv[...].astype(bf16).reshape(SEQ, 64, 128)


def owner_order(core):
    src, dst = iota((D, 1024), 0), iota((D, 1024), 1)
    half = dst >> 9
    s = (dst >> 5) & 15
    y = (dst >> 3) & 3
    j = dst & 7
    which = jnp.where(half == 0, core, 1 - core)
    col = (2 * y + which) * 96 + s * 6 + j
    return ((src == col) & (j < 6)).astype(f32).astype(bf16)


S_MID, S_GI, S_INNER, S_GO, S_ATT, S_GA, S_END = 0, 512, 3584, 5120, 5888, 6400, 7168


def middle_kernel(
    info, recv, hidden, vecs, cot, out_w, inner_w, outer_w,
    act_out, grad_att_out, gmi_out, send_out, own_out, small_out,
    act, slope,
):
    core = info[3]
    keep = info[4].astype(f32)
    att = jnp.concatenate(
        [jnp.concatenate([recv[u * PAIRS + p] for p in range(PAIRS)], axis=1) for u in range(2)], axis=0
    )
    middle_in = hidden[...] + nn(att, out_w[...]) + vec(vecs, R_OUT_B)
    xm, rm = stats(middle_in)
    middle = xm * vec(vecs, R_MID_G) + vec(vecs, R_MID_S)
    middle_b = middle.astype(bf16)
    outer = jnp.zeros((ROWS, D), f32)
    for q in range(4):
        cols = slice(q * D, (q + 1) * D)
        pre = nn(middle_b, inner_w[:, cols]) + vec(vecs, R_INNER_B + q)
        c = cdf(pre)
        inner_b = (pre * c).astype(bf16)
        act[:, cols] = inner_b
        slope[:, cols] = c + pre * (0.3989422804014327 * jnp.exp(-0.5 * pre * pre))
        outer += nn(inner_b, outer_w[cols, :])
    final_in = middle + keep * (outer + vec(vecs, R_OUTER_B))
    xf, rf = stats(final_in)
    act_out[...] = (xf * vec(vecs, R_FIN_G) + vec(vecs, R_FIN_S)).astype(bf16)
    gfi, fin_g, fin_s = norm_back(xf, rf, vec(vecs, R_FIN_G), cot[...].astype(f32))
    grad_outer = (keep * gfi).astype(bf16)
    grad_middle = gfi
    for q in range(4):
        cols = slice(q * D, (q + 1) * D)
        grad_inner = (slope[:, cols] * nt(grad_outer, outer_w[cols, :])).astype(bf16)
        send_out[:, S_GI + q * D : S_GI + (q + 1) * D] = grad_inner
        small_out[3 + q : 4 + q, :] = col_sum(grad_inner)
        grad_middle += nt(grad_inner, inner_w[:, cols])
    gmi, mid_g, mid_s = norm_back(xm, rm, vec(vecs, R_MID_G), grad_middle)
    gmi_out[...] = gmi
    grad_attn = gmi.astype(bf16)
    grad_att = nt(grad_attn, out_w[...]).astype(bf16)
    for u in range(2):
        for p in range(PAIRS):
            grad_att_out[u * PAIRS + p] = grad_att[u * 64 : (u + 1) * 64, p * 128 : (p + 1) * 128]
    grad_att_out[2 * PAIRS :] = jnp.zeros((SEQ - 2 * PAIRS, 64, 128), bf16)
    for row, value in ((0, fin_g), (1, fin_s), (2, col_sum(grad_outer)), (7, mid_g), (8, mid_s), (9, col_sum(grad_attn))):
        small_out[row : row + 1, :] = value
    small_out[10:16, :] = jnp.zeros((6, D), f32)
    order = owner_order(core)
    mid = nn(middle_b, order).astype(bf16)
    att_p = nn(att, order).astype(bf16)
    own_out[:, 0:512] = mid[:, :512]
    own_out[:, 2048:2560] = att_p[:, :512]
    send_out[:, S_MID : S_MID + 512] = mid[:, 512:]
    send_out[:, S_ATT : S_ATT + 512] = att_p[:, 512:]
    send_out[:, S_GO : S_GO + D] = grad_outer
    send_out[:, S_GA : S_GA + D] = grad_attn
    first = core == 0
    for y in range(4):
        even = act[:, 2 * y * 384 : (2 * y + 1) * 384]
        odd = act[:, (2 * y + 1) * 384 : (2 * y + 2) * 384]
        own_out[:, 512 + y * 384 : 512 + (y + 1) * 384] = jnp.where(first, even, odd)
        send_out[:, S_INNER + y * 384 : S_INNER + (y + 1) * 384] = jnp.where(first, odd, even)


def dense_grads_kernel(own, sent, got, out):
    def right(start, width):
        return jnp.concatenate([sent[:, start : start + width], got[:, start : start + width]], axis=0)

    def left(start, theirs, width):
        return jnp.concatenate([own[:, start : start + width], got[:, theirs : theirs + width]], axis=0)

    mid = left(0, S_MID, 512)
    for half in range(2):
        res = [tn(mid, right(S_GI + (2 * half + k) * D, D)) for k in range(2)]
        for n in range(64):
            pair = jnp.concatenate([r[n * 8 : n * 8 + 8] for r in res], axis=0)
            out[n * 64 + half * 16 : n * 64 + half * 16 + 16, :] = pair.astype(bf16)
    outer = tn(left(512, S_INNER, 1536), right(S_GO, D))
    output = tn(left(2048, S_ATT, 512), right(S_GA, D))
    for s in range(16):
        for y in range(4):
            n = s * 4 + y
            both = jnp.concatenate(
                [outer[y * 384 + s * 24 : y * 384 + s * 24 + 24], output[n * 8 : n * 8 + 8]], axis=0
            )
            out[n * 64 + 32 : n * 64 + 64, :] = both.astype(bf16)


def qkv_back_kernel(
    info, recv, gmi, pre_in, masked, vecs, weight, summed_out, conv_out, send_out, own_out, small_out, scratch
):
    pre = pre_in[...]
    xhat, r = stats(masked[...] + gelu(pre))
    hidden_b = (xhat * vec(vecs, R_ENC_G) + vec(vecs, R_ENC_S)).astype(bf16)
    grad_hidden = gmi[...]
    sums = []
    for slot in range(3):
        part = jnp.concatenate(
            [
                jnp.concatenate([recv[u * PAIRS + p, slot * 64 : (slot + 1) * 64, :] for p in range(PAIRS)], axis=1)
                for u in range(2)
            ],
            axis=0,
        )
        send_out[:, 512 + slot * D : 512 + (slot + 1) * D] = part
        sums.append(col_sum(part))
        grad_hidden += nt(part, weight[:, slot * D : (slot + 1) * D])
    grad_summed, enc_g, enc_s = norm_back(xhat, r, vec(vecs, R_ENC_G), grad_hidden)
    summed_out[...] = grad_summed
    grad_conv = (gelu_slope(pre) * grad_summed).astype(bf16).astype(f32)
    rows_to_groups(grad_conv, scratch, conv_out)
    for row, value in enumerate((enc_g, enc_s, sums[0], sums[2], jnp.sum(grad_conv, axis=0, keepdims=True))):
        small_out[row : row + 1, :] = value
    small_out[5:8, :] = jnp.zeros((3, D), f32)
    hid = nn(hidden_b, owner_order(info[3])).astype(bf16)
    own_out[...] = hid[:, :512]
    send_out[:, :512] = hid[:, 512:]


def qkv_grad_kernel(own, sent, got, out):
    left = jnp.concatenate([own[...], got[:, :512]], axis=0)
    res = [
        tn(left, jnp.concatenate([x[:, 512 + q * D : 512 + (q + 1) * D] for x in (sent, got)], axis=0))
        for q in range(3)
    ]
    for n in range(0, 64, 2):
        rows = [r[m * 8 : m * 8 + 8] for m in (n, n + 1) for r in res]
        out[n * 24 : n * 24 + 48, :] = jnp.concatenate(rows, axis=0).astype(bf16)


def feats_back_kernel(
    info, conv, summed, feats, vecs, weight, small_a, small_b, feats_out, tail_out, rows, spread
):
    grad_proj = ((summed[...] + groups_to_rows(conv, rows)) * live_rows(info)).astype(bf16)
    xhat, r = stats(feats[...].astype(f32))
    normed = (xhat * vec(vecs, R_IN_G, C_IN) + vec(vecs, R_IN_S, C_IN)).astype(bf16)
    grad_feats, in_g, in_s = norm_back(xhat, r, vec(vecs, R_IN_G, C_IN), nt(grad_proj, weight[...]))
    feats_out[...] = grad_feats
    proj = tn(normed, grad_proj)
    upper = iota((8, 384), 0) < 4
    for n in range(0, 128, 2):
        a, b = proj[n * 4 : n * 4 + 8, :384], proj[n * 4 : n * 4 + 8, 384:]
        both = jnp.concatenate(
            [jnp.where(upper, a, pltpu.roll(b, 4, 0)), jnp.where(upper, pltpu.roll(a, 4, 0), b)], axis=0
        )
        tail_out[n * 8 : n * 8 + 16, :384] = both.astype(bf16)
    a = lambda k: small_a[k : k + 1, :]
    b = lambda k: small_b[k : k + 1, :]
    vectors = [col_sum(grad_proj), b(4), b(0), b(1), b(2), b(3), a(9), a(7), a(8), a(2), a(0), a(1)]
    lane = iota((8, D), 1)
    sub = iota((8, D), 0)
    slot6 = lane - 6 * int_div(lane, 6)
    main = jnp.concatenate([jnp.where(slot6 == sub, v, 0.0) for v in vectors] + [jnp.zeros((32, D), f32)], axis=0)
    lane24, sub24 = iota((24, D), 1), iota((24, D), 0)
    slot24 = lane24 - 24 * int_div(lane24, 24)
    inner = [
        jnp.concatenate(
            [jnp.zeros((96, D), f32), jnp.where(slot24 == sub24, a(3 + k), 0.0), jnp.zeros((8, D), f32)], axis=0
        )
        for k in range(4)
    ]
    lane4, sub4 = iota((8, C_IN), 1) & 3, iota((8, C_IN), 0)
    last = jnp.concatenate(
        [
            jnp.zeros((120, C_IN), f32),
            jnp.where(lane4 == sub4, in_g, 0.0) + jnp.where(lane4 == sub4 - 4, in_s, 0.0),
        ],
        axis=0,
    )
    own = iota((128, D), 0)
    col = iota((128, D), 1)
    pick6 = (int_div(col, 6) == own).astype(f32).astype(bf16)
    pick24 = [(int_div(col, 24) + 32 * k == own).astype(f32).astype(bf16) for k in range(4)]
    pick4 = ((iota((128, C_IN), 1) >> 2) == iota((128, C_IN), 0)).astype(f32).astype(bf16)
    spread[...] = jnp.zeros_like(spread)
    terms = [(pick6, main)] + list(zip(pick24, inner)) + [(pick4, last)]
    high = [(p, m.astype(bf16)) for p, m in terms]
    low = [(p, (m - h.astype(f32)).astype(bf16)) for (p, m), (_, h) in zip(terms, high)]
    for k, part in enumerate((high, low)):
        spread[pl.ds(k, 128, stride=8), :] = functools.reduce(lambda x, y: x + y, [nt(p, m) for p, m in part])
    tail_out[:, 384:] = spread[...].astype(bf16)


def to_peers(x, axis, groups=None):
    return lax.all_to_all(x, axis, 0, 0, tiled=True, axis_index_groups=groups)


Y_GROUPS = [[0, 2, 4, 6], [1, 3, 5, 7]]


def local(
    feats, lengths, skip_flag, cotangent, input_gain, input_shift, proj_weight, proj_bias, conv_weight, conv_bias,
    encoder_gain, encoder_shift, qkv_weight, query_bias, value_bias, output_weight, output_bias, middle_gain,
    middle_shift, inner_weight, inner_bias, outer_weight, outer_bias, final_gain, final_shift,
):
    seq = lax.axis_index("seq")
    core = lax.axis_index("batch") % 2
    pad = jnp.zeros((D - C_IN,), bf16)
    vecs = (
        jnp.concatenate(
            [
                input_gain, pad, input_shift, pad, proj_bias, conv_bias, encoder_gain, encoder_shift, query_bias,
                value_bias, output_bias, middle_gain, middle_shift, inner_bias, outer_bias, final_gain, final_shift,
            ]
        )
        .astype(f32)
        .reshape(18, D)
    )
    attend_len = jnp.where(seq < PAIRS, lengths[0], lengths[1])
    info = jnp.stack([lengths[0], lengths[1], seq, core, 1 - skip_flag[0], attend_len]).astype(i32)
    rows_in = feats.reshape(ROWS, C_IN)
    cot = cotangent.reshape(ROWS, D)

    normed, masked, conv_send = call(
        project_kernel,
        [shape((ROWS, C_IN), bf16), shape((ROWS, D), f32), shape((ROWS, D), bf16)],
        info, rows_in, vecs, proj_weight, smem=(0,), flops=2 * ROWS * C_IN * D, name="project",
        scratch=[TRANSPOSE_SCRATCH],
    )
    conv_x = to_peers(conv_send, "seq")
    own_taps = lax.dynamic_slice_in_dim(conv_weight, seq * GW, GW, axis=0)
    taps = own_taps.transpose(0, 2, 1).reshape(GW, KW * GW)
    (band,) = call(toeplitz_kernel, [shape((D, TAP_BLOCKS * D), bf16)], taps, flops=10**7, name="toeplitz")

    whole = pl.BlockSpec((ROWS, D), lambda i: (0, 0))
    band_block = pl.BlockSpec((D, D), lambda i: (0, i))
    (conv_y,) = call(
        conv_kernel, [shape((ROWS, D), bf16)], conv_x, band, grid=(TAP_BLOCKS,), in_specs=[whole, band_block],
        out_specs=[whole], scratch=[pltpu.VMEM((ROWS, D), f32)], flops=2 * ROWS * D * D * TAP_BLOCKS, name="conv",
    )
    conv_back = to_peers(conv_y, "seq")
    conv_pre, hidden, qkv_send = call(
        qkv_kernel,
        [shape((ROWS, D), f32), shape((ROWS, D), f32), shape((SEQ, 192, 128), bf16)],
        conv_back, masked, vecs, qkv_weight, flops=2 * ROWS * D * 3 * D, name="qkv", scratch=[TRANSPOSE_SCRATCH],
    )
    qkv = to_peers(qkv_send, "seq")
    attended, logs = call(
        attend_kernel,
        [shape((1024, 128), bf16), shape((1024, 128), f32)],
        info, qkv, smem=(0,), flops=8 * 1024 * 1024 * 128, name="attend",
    )
    att_recv = to_peers(attended.reshape(SEQ, 64, 128), "seq")
    activations, grad_att_send, gmi, pair_send, pair_own, small_a = call(
        middle_kernel,
        [
            shape((ROWS, D), bf16), shape((SEQ, 64, 128), bf16), shape((ROWS, D), f32), shape((ROWS, S_END), bf16),
            shape((ROWS, 2560), bf16), shape((16, D), f32),
        ],
        info, att_recv, hidden, vecs, cot, output_weight, inner_weight, outer_weight, smem=(0,),
        scratch=[pltpu.VMEM((ROWS, FF), bf16), pltpu.VMEM((ROWS, FF), f32)],
        flops=2 * ROWS * (4 * D * FF + 2 * D * D), name="middle",
    )
    swap = [(i, i ^ 1) for i in range(8)]
    pair_got = lax.ppermute(pair_send, "batch", swap)
    grad_att = to_peers(grad_att_send, "seq").reshape(1024, 128)
    (dense,) = call(
        dense_grads_kernel, [shape((4096, D), bf16)], pair_own, pair_send, pair_got,
        flops=2 * 256 * D * (2048 + 1536 + 512), name="dense_grads",
    )
    dense_part = lax.psum_scatter(dense, "seq", scatter_dimension=0, tiled=True)
    dense_own = lax.psum_scatter(
        dense_part, "batch", scatter_dimension=0, tiled=True, axis_index_groups=Y_GROUPS
    ).astype(f32)

    (grad_qkv_send,) = call(
        attend_back_kernel, [shape((SEQ, 192, 128), bf16)], info, qkv, grad_att, logs, smem=(0,),
        scratch=[pltpu.VMEM((1024, 128), f32)] * 2, flops=20 * 1024 * 1024 * 128, name="attend_back",
    )
    grad_qkv = to_peers(grad_qkv_send, "seq")
    grad_summed, grad_conv_send, qkv_pair_send, qkv_pair_own, small_b = call(
        qkv_back_kernel,
        [
            shape((ROWS, D), f32), shape((ROWS, D), bf16), shape((ROWS, 512 + 3 * D), bf16), shape((ROWS, 512), bf16),
            shape((8, D), f32),
        ],
        info, grad_qkv, gmi, conv_pre, masked, vecs, qkv_weight, smem=(0,), scratch=[TRANSPOSE_SCRATCH],
        flops=2 * ROWS * D * 3 * D, name="qkv_back",
    )
    grad_conv = to_peers(grad_conv_send, "seq")
    qkv_pair_got = lax.ppermute(qkv_pair_send, "batch", swap)
    (qkv_grads,) = call(
        qkv_grad_kernel, [shape((1536, D), bf16)], qkv_pair_own, qkv_pair_send, qkv_pair_got,
        flops=2 * 256 * 512 * 3 * D, name="qkv_grads",
    )
    (grad_x,) = call(
        conv_back_kernel, [shape((ROWS, D), bf16)], grad_conv, band, grid=(TAP_BLOCKS,), in_specs=[whole, band_block],
        out_specs=[whole], scratch=[pltpu.VMEM((ROWS, D), f32)], flops=2 * ROWS * D * D * TAP_BLOCKS,
        name="conv_back",
    )
    grad_x_back = to_peers(grad_x, "seq")
    (tap_grads,) = call(
        conv_weight_kernel, [shape((8 * GW, D), f32)], grad_conv, conv_x, grid=(TAP_BLOCKS,), in_specs=[whole, whole],
        out_specs=[pl.BlockSpec((8 * GW, D), lambda i: (0, 0))], scratch=[pltpu.VMEM((TAP_BLOCKS, GW, D), f32), pltpu.VMEM((8 * GW, 128), f32)],
        flops=2 * ROWS * D * D * TAP_BLOCKS, name="conv_grads",
    )
    tap_part = lax.psum_scatter(tap_grads, "batch", scatter_dimension=0, tiled=True)
    moves = [(b * 16 + g, (g // 2) * 16 + 8 * (g % 2) + b) for b in range(8) for g in range(16)]
    tap_own = lax.ppermute(tap_part, ("batch", "seq"), moves)
    grad_conv_weight = tap_own.reshape(6, KW, GW).transpose(0, 2, 1)

    qkv_part = jnp.sum(to_peers(qkv_grads, "seq").reshape(SEQ, 96, D).astype(f32), axis=0).astype(bf16)
    qkv_own = jnp.sum(to_peers(qkv_part, "batch", Y_GROUPS).reshape(4, 24, D).astype(f32), axis=0)

    grad_feats, tail = call(
        feats_back_kernel,
        [shape((ROWS, C_IN), f32), shape((1024, 512), bf16)],
        info, grad_x_back, grad_summed, rows_in, vecs, proj_weight, small_a, small_b, smem=(0,),
        scratch=[TRANSPOSE_SCRATCH, pltpu.VMEM((1024, 128), f32)], flops=4 * ROWS * C_IN * D,
        name="feats_back",
    )
    tail_sum = jnp.sum(to_peers(tail, ("batch", "seq")).reshape(128, 8, 512).astype(f32), axis=0)
    grad_proj_weight = jnp.concatenate([tail_sum[:4, :384], tail_sum[4:, :384]], axis=1)
    small = tail_sum[0, 384:] + tail_sum[1, 384:]
    (
        g_proj_b, g_conv_b, g_enc_g, g_enc_s, g_q_b, g_v_b, g_out_b, g_mid_g, g_mid_s, g_outer_b, g_fin_g, g_fin_s,
    ) = [small[8 * k : 8 * k + 6] for k in range(12)]

    def heads(x, parts):
        return x.reshape(parts, 8, D)[:, :6].transpose(1, 0, 2).reshape(6, parts * D)

    return (
        activations.reshape(2, 64, D),
        grad_feats.reshape(2, 64, C_IN),
        small[120:124],
        small[124:128],
        grad_proj_weight,
        g_proj_b,
        grad_conv_weight,
        g_conv_b,
        g_enc_g,
        g_enc_s,
        heads(qkv_own, 3),
        g_q_b,
        g_v_b,
        dense_own[56:62],
        g_out_b,
        g_mid_g,
        g_mid_s,
        heads(dense_own[:32], 4),
        small[96:120],
        dense_own[32:56],
        g_outer_b,
        g_fin_g,
        g_fin_s,
    )


def solution(mesh):
    split = P("batch", "seq", None)
    both = ("batch", "seq")
    placed = (split, P("batch"), P("batch"), split) + (P(),) * 21
    row, matrix = P(both), P(both, None)
    return jax.shard_map(
        local,
        mesh=mesh,
        in_specs=placed,
        out_specs=(
            split, split, row, row, matrix, row, P(both, None, None), row, row, row, matrix, row, row, matrix, row,
            row, row, matrix, row, matrix, row, row, row,
        ),
        check_vma=False,
    )
```

time: 3220 us -> 325 us (0.10); the launches traced: 3170 us -> 323 us
  local copies, waits for them, and re-layouts: 2450 us -> 31.9 us
  waiting for transfers between devices: 432 us -> 37.7 us
  other arithmetic: 133 us -> 3.37 us
  matrix products: 128 us -> 0 us
  blocking collectives: 0 us -> 96.4 us
  Pallas kernels: 0 us -> 95.9 us
    another operation x278 -> x1, local copies, waits for them, and re-layouts: 801 us -> 1.25 us  [local(): jnp.stack([lengths[0], lengths[1], seq, core, 1 - skip_flag[0], attend_len])]
    unnamed x742 -> x27, local copies, waits for them, and re-layouts: 598 us -> 16.9 us
    transpose x18 -> x2, local copies, waits for them, and re-layouts: 476 us -> 1.95 us  [local(): taps = own_taps.transpose(0, 2, 1).reshape(GW, KW * GW)]
    unnamed x6 -> x3, waiting for transfers between devices: 360 us -> 0.05 us
    reshape x45 -> x3, local copies, waits for them, and re-layouts: 273 us -> 4.41 us  [the longest x1 3.58 us: local(): taps = own_taps.transpose(0, 2, 1).reshape(GW, KW * GW)]
    slice x22 -> x7, local copies, waits for them, and re-layouts: 112 us -> 5.83 us  [the longest x1 1.41 us: local(): dense_own[32:56]]
    squeeze x16 -> x0, local copies, waits for them, and re-layouts: 103 us -> none  [conv_apply(): arranged[tap_block]]
    dot_general x37 -> x0, matrix products: 97.5 us -> none  [the longest x16 23.5 us: conv_apply(): jnp.einsum('rgi,gio->rgo', window, arranged[tap_block], preferred_element...]
  transfers between devices with their start and end apart: 9 -> 10, of which waited for: 3 -> 6; matrix products, arithmetic and copies ran while one was open for 49% -> 3% of each run, Pallas kernels for 0% -> 16%
where the time goes in v1:
time: 325 us; the launch traced here: 323 us
  blocking collectives  96.4 us (30%)
  Pallas kernels  95.9 us (30%)
  starting transfers between devices  41.9 us (13%)
  waiting for transfers between devices  37.7 us (12%)
  local copies, waits for them, and re-layouts  31.9 us (10%)
  between operations  15.9 us (5%)
  other arithmetic  3.37 us (1%)
    all_to_all x7, blocking collectives, to_peers(): return lax.all_to_all(x, axis, 0, 0, tiled=True, axis_index_groups=groups)  96.4 us
    pallas_call x13, Pallas kernels, call(): pl.pallas_call(body, out_shape=out_shapes, in_specs=in_specs or specs, ou...  95.9 us
    all_to_all x4, starting transfers between devices, to_peers(): return lax.all_to_all(x, axis, 0, 0, tiled=True, axis_index_groups=groups)  28.8 us
    unnamed x27, local copies, waits for them, and re-layouts  16.9 us
    reduce_scatter x1, waiting for transfers between devices, local(): lax.psum_scatter(tap_grads, 'batch', scatter_dimension=0, tiled=True)  15.7 us
    all_to_all x4, waiting for transfers between devices, to_peers(): return lax.all_to_all(x, axis, 0, 0, tiled=True, axis_index_groups=groups)  12.8 us
    ppermute x1, starting transfers between devices, local(): tap_own = lax.ppermute(tap_part, ('batch', 'seq'), moves)  6.59 us
  transfers between devices with their start and end apart: 10, of which 6 were waited for; matrix products, arithmetic and copies ran while one was open for 3% of the time, Pallas kernels for 16%

profile of v1, /device:TPU:1, one launch (start us, length us, event | category | flops | bytes accessed | tf_op | source)
XLA Modules:
  0.0 323.1 jit_solution(9568052649879016020)
XLA Ops:
  25.6 2.6 project.1
  28.2 8.4 %all-to-all-start = ((bf16[16,8,768]{2,1,0:T(8,128)(2,1)}), bf16[16,8,768]{2,1,0:T(8,128)(2,1)S(1)}, u32[]{:S(2)}, u32[]{:S(2)}) async-start(bf16[16,8,768]{2,1,0:T(8,128)(2,1)} %bitcast.81), calls=%async_computation | async-start | bytes 393216 | tf_op jit(solution)/shard_map/all_to_all | solution.py:530
  38.7 3.6 %reshape.126.taps = bf16[48,6144]{1,0:T(8,128)(2,1)} reshape(bf16[48,128,48]{2,1,0:T(8,128)(2,1)S(1)} %copy.52) | data formatting | bytes 1179648 | tf_op jit(solution)/shard_map/reshape | solution.py:567
  42.3 6.4 %toeplitz.1.w = bf16[768,6912]{1,0:T(8,128)(2,1)} custom-call(bf16[48,6144]{1,0:T(8,128)(2,1)} %reshape.126.taps), custom_call_target="tpu_custom_call" | custom-call | flops 10000000 | bytes 11206656 | tf_op jit(solution)/shard_map/toeplitz/pallas_call | solution.py:143
  49.3 10.4 %conv.1 = bf16[128,768]{1,0:T(8,128)(2,1)} custom-call(bf16[128,768]{1,0:T(8,128)(2,1)} %bitcast.71, bf16[768,6912]{1,0:T(8,128)(2,1)} %toeplitz.1.w), custom_call_target="tpu_custom_call" | custom-call | flops 1358954496 | bytes 11010048 | tf_op jit(solution)/shard_map/conv/pallas_call | solution.py:143
  59.7 13.7 %all_to_all.91 = bf16[16,8,768]{2,1,0:T(8,128)(2,1)} all-to-all(bf16[16,8,768]{2,1,0:T(8,128)(2,1)} %bitcast.76), channel_id=1, replica_groups=mesh['batch'=8,'seq'=16] {'seq'}, dimensions={0} | all-to-all | bytes 393216 | tf_op jit(solution)/shard_map/all_to_all | solution.py:530
  73.4 4.3 %qkv.1 = (f32[128,768]{1,0:T(8,128)}, f32[128,768]{1,0:T(8,128)}, bf16[16,192,128]{2,1,0:T(8,128)(2,1)}) custom-call(bf16[128,768]{1,0:T(8,128)(2,1)} %bitcast.69, f32[128,768]{1,0:T(8,128)} %get-tuple-element.44.masked, f32[18,768]{1,0:T(8,128)} %reshape.137.vecs, bf16[768,2304]{1,0:T(8,128)(2,1)} %weight.6), custom_call_target="tpu_custom_call" | custom-call | flops 452984832 | bytes 5756928 | tf_op jit(solution)/shard_map/qkv/pallas_call | solution.py:143
  77.7 15.2 %all_to_all.92.qkv = bf16[16,192,128]{2,1,0:T(8,128)(2,1)} all-to-all(bf16[16,192,128]{2,1,0:T(8,128)(2,1)} %get-tuple-element.45), channel_id=1, replica_groups=mesh['batch'=8,'seq'=16] {'seq'}, dimensions={0} | all-to-all | bytes 1572864 | tf_op jit(solution)/shard_map/all_to_all | solution.py:530
  92.9 7.6 %attend.1 = (bf16[1024,128]{1,0:T(8,128)(2,1)}, f32[1024,128]{1,0:T(8,128)}) custom-call(s32[6]{0:T(128)} %stack.16.info, bf16[16,192,128]{2,1,0:T(8,128)(2,1)} %all_to_all.92.qkv), custom_call_target="tpu_custom_call" | custom-call | flops 1073741824 | bytes 1572888 | tf_op jit(solution)/shard_map/attend/pallas_call | solution.py:143
  100.5 11.5 %all_to_all.93.recv = bf16[16,64,128]{2,1,0:T(8,128)(2,1)} all-to-all(bf16[16,64,128]{2,1,0:T(8,128)(2,1)} %bitcast.80), channel_id=1, replica_groups=mesh['batch'=8,'seq'=16] {'seq'}, dimensions={0} | all-to-all | bytes 524288 | tf_op jit(solution)/shard_map/all_to_all | solution.py:530
  112.0 12.6 %middle.1 = (bf16[128,768]{1,0:T(8,128)(2,1)}, bf16[16,64,128]{2,1,0:T(8,128)(2,1)}, f32[128,768]{1,0:T(8,128)}, bf16[128,7168]{1,0:T(8,128)(2,1)}, bf16[128,2560]{1,0:T(8,128)(2,1)}, /*index=5*/f32[16,768]{1,0:T(8,128)}) custom-call(s32[6]{0:T(128)} %stack.16.info, bf16[16,64,128]{2,1,0:T(8,128)(2,1)} %all_to_all.93.recv, ...), custom_call_target="tpu_custom_call" | custom-call | flops 2717908992 | bytes 14915608 | tf_op jit(solution)/shard_map/middle/pallas_call | solution.py:143
  124.6 5.3 %collective-permute-start.2 = (bf16[128,7168]{1,0:T(8,128)(2,1)}, bf16[128,7168]{1,0:T(8,128)(2,1)S(1)}, u32[]{:S(2)}, u32[]{:S(2)}) collective-permute-start(bf16[128,7168]{1,0:T(8,128)(2,1)} %get-tuple-element.62.sent), channel_id=1, source_target_pairs={{0,16},{16,0},{32,48},{48,32},{64,80},{80,64},{96,112},{112,96},{1... | collective-permute-start | bytes 5505032 | tf_op jit(solution)/shard_map/ppermute | solution.py:600
  129.9 3.6 %collective-permute-done.2.got = bf16[128,7168]{1,0:T(8,128)(2,1)S(1)} collective-permute-done((bf16[128,7168]{1,0:T(8,128)(2,1)}, bf16[128,7168]{1,0:T(8,128)(2,1)S(1)}, u32[]{:S(2)}, u32[]{:S(2)}) %collective-permute-start.2) | collective-permute-done | bytes 1835040 | tf_op jit(solution)/shard_map/ppermute | solution.py:600
  134.7 6.7 %dense_grads.1 = bf16[4096,768]{1,0:T(8,128)(2,1)} custom-call(bf16[128,2560]{1,0:T(8,128)(2,1)} %get-tuple-element.61.own, bf16[128,7168]{1,0:T(8,128)(2,1)} %get-tuple-element.62.sent, bf16[128,7168]{1,0:T(8,128)(2,1)} %copy-done), custom_call_target="tpu_custom_call" | custom-call | flops 1610612736 | bytes 10616832 | tf_op jit(solution)/shard_map/dense_grads/pallas_call | solution.py:143
  142.4 10.9 %all_to_all.94 = bf16[16,64,128]{2,1,0:T(8,128)(2,1)} all-to-all(bf16[16,64,128]{2,1,0:T(8,128)(2,1)S(1)} %copy-done.4), channel_id=1, replica_groups=mesh['batch'=8,'seq'=16] {'seq'}, dimensions={0} | all-to-all | bytes 524288 | tf_op jit(solution)/shard_map/all_to_all | solution.py:530
  153.3 11.3 %attend_back.1 = bf16[16,192,128]{2,1,0:T(8,128)(2,1)} custom-call(s32[6]{0:T(128)} %stack.16.info, bf16[16,192,128]{2,1,0:T(8,128)(2,1)} %all_to_all.92.qkv, bf16[1024,128]{1,0:T(8,128)(2,1)} %bitcast.79, f32[1024,128]{1,0:T(8,128)} %get-tuple-element.50.logs), custom_call_target="tpu_custom_call" | custom-call | flops 2684354560 | bytes 2359320 | tf_op jit(solution)/shard_map/attend_back/pallas_call | solution.py:143
  164.6 21.1 %all_to_all.95.recv = bf16[16,192,128]{2,1,0:T(8,128)(2,1)} all-to-all(bf16[16,192,128]{2,1,0:T(8,128)(2,1)} %attend_back.1), channel_id=1, replica_groups=mesh['batch'=8,'seq'=16] {'seq'}, dimensions={0} | all-to-all | bytes 1572864 | tf_op jit(solution)/shard_map/all_to_all | solution.py:530
  185.7 5.7 %qkv_back.1 = (f32[128,768]{1,0:T(8,128)}, bf16[128,768]{1,0:T(8,128)(2,1)}, bf16[128,2816]{1,0:T(8,128)(2,1)}, bf16[128,512]{1,0:T(8,128)(2,1)}, f32[8,768]{1,0:T(8,128)}) custom-call(s32[6]{0:T(128)} %stack.16.info, bf16[16,192,128]{2,1,0:T(8,128)(2,1)} %all_to_all.95.recv, f32[128,768]{1,0:T(8,128)} %get-tuple-element.51.gmi, ...), custom_call_target="tpu_custom_call" | custom-call | flops 452984832 | bytes 7026712 | tf_op jit(solution)/shard_map/qkv_back/pallas_call | solution.py:143
  191.4 12.2 %all_to_all.96 = bf16[16,8,768]{2,1,0:T(8,128)(2,1)} all-to-all(bf16[16,8,768]{2,1,0:T(8,128)(2,1)} %bitcast.82), channel_id=1, replica_groups=mesh['batch'=8,'seq'=16] {'seq'}, dimensions={0} | all-to-all | bytes 393216 | tf_op jit(solution)/shard_map/all_to_all | solution.py:530
  203.5 9.6 %conv_back.1 = bf16[128,768]{1,0:T(8,128)(2,1)} custom-call(bf16[128,768]{1,0:T(8,128)(2,1)} %bitcast.73, bf16[768,6912]{1,0:T(8,128)(2,1)} %toeplitz.1.w), custom_call_target="tpu_custom_call" | custom-call | flops 1358954496 | bytes 11010048 | tf_op jit(solution)/shard_map/conv_back/pallas_call | solution.py:143
  213.1 11.8 %all_to_all.97 = bf16[16,8,768]{2,1,0:T(8,128)(2,1)} all-to-all(bf16[16,8,768]{2,1,0:T(8,128)(2,1)} %bitcast.75), channel_id=1, replica_groups=mesh['batch'=8,'seq'=16] {'seq'}, dimensions={0} | all-to-all | bytes 393216 | tf_op jit(solution)/shard_map/all_to_all | solution.py:530
  224.9 4.2 %feats_back.1 = (f32[128,512]{1,0:T(8,128)}, bf16[1024,512]{1,0:T(8,128)(2,1)}) custom-call(s32[6]{0:T(128)} %stack.16.info, bf16[128,768]{1,0:T(8,128)(2,1)} %bitcast.70, f32[128,768]{1,0:T(8,128)} %get-tuple-element.54.summed, bf16[128,512]{1,0:T(8,128)(2,1)} %bitcast.78, f32[18,768]{1,0:T(8,128)} %reshape.137.vecs, bf16[512,768]{1,0:T(8,128)(2,1)} %weight.7, ...), custom_call_target="tpu_custom_call" | custom-call | flops 201326592 | bytes 2947096 | tf_op jit(solution)/shard_map/feats_back/pallas_call | solution.py:143
  229.1 10.6 %all-to-all-start.8 = ((bf16[128,8,512]{2,1,0:T(8,128)(2,1)}), bf16[128,8,512]{2,1,0:T(8,128)(2,1)S(1)}, u32[]{:S(2)}, u32[]{:S(2)}) async-start(bf16[128,8,512]{2,1,0:T(8,128)(2,1)} %bitcast.68), calls=%async_computation.8 | async-start | bytes 2097152 | tf_op jit(solution)/shard_map/all_to_all | solution.py:530
  239.8 11.1 %conv_grads.1 = f32[384,768]{1,0:T(8,128)} custom-call(bf16[128,768]{1,0:T(8,128)(2,1)} %bitcast.74, bf16[128,768]{1,0:T(8,128)(2,1)} %bitcast.72), custom_call_target="tpu_custom_call" | custom-call | flops 1358954496 | bytes 1572864 | tf_op jit(solution)/shard_map/conv_grads/pallas_call | solution.py:143
  254.7 3.6 %qkv_grads.1 = bf16[1536,768]{1,0:T(8,128)(2,1)} custom-call(bf16[128,512]{1,0:T(8,128)(2,1)} %get-tuple-element.59.own, bf16[128,2816]{1,0:T(8,128)(2,1)} %get-tuple-element.60.sent, bf16[128,2816]{1,0:T(8,128)(2,1)} %copy-done.3), custom_call_target="tpu_custom_call" | custom-call | flops 603979776 | bytes 3932160 | tf_op jit(solution)/shard_map/qkv_grads/pallas_call | solution.py:143
  258.4 6.4 %all-to-all-start.9 = ((bf16[16,96,768]{2,1,0:T(8,128)(2,1)}), bf16[16,96,768]{2,1,0:T(8,128)(2,1)S(1)}, u32[]{:S(2)}, u32[]{:S(2)}) async-start(bf16[16,96,768]{2,1,0:T(8,128)(2,1)} %bitcast.66), calls=%async_computation.10 | async-start | bytes 4718592 | tf_op jit(solution)/shard_map/all_to_all | solution.py:530
  266.3 15.7 %reduce-scatter.4.cloned.1.call-done = f32[48,768]{1,0:T(8,128)} async-done(((f32[384,768]{1,0:T(8,128)}), f32[48,768]{1,0:T(8,128)}) %reduce-scatter.4.cloned.1.call-update) | async-done | bytes 147472 | tf_op jit(solution)/shard_map/reduce_scatter | solution.py:642
  282.0 6.6 %collective-permute-start = (f32[48,768]{1,0:T(8,128)}, f32[48,768]{1,0:T(8,128)S(1)}, u32[]{:S(2)}, u32[]{:S(2)}) collective-permute-start(f32[48,768]{1,0:T(8,128)} %reduce-scatter.4.cloned.1.call-done), channel_id=1, source_target_pairs={{0,0},{1,8},{2,16},{3,24},{4,32},{5,40},{6,48},{7,56},{8,64},{9,72... | collective-permute-start | bytes 442376 | tf_op jit(solution)/shard_map/ppermute | solution.py:644
  289.2 8.3 %all-to-all-done.9 = bf16[16,96,768]{2,1,0:T(8,128)(2,1)S(1)} async-done(((bf16[16,96,768]{2,1,0:T(8,128)(2,1)}), bf16[16,96,768]{2,1,0:T(8,128)(2,1)S(1)}, u32[]{:S(2)}, u32[]{:S(2)}) %all-to-all-start.9) | async-done | bytes 2359328 | tf_op jit(solution)/shard_map/all_to_all | solution.py:530
  298.5 3.3 %all-to-all-start.10 = ((bf16[4,24,768]{2,1,0:T(8,128)(2,1)}), bf16[4,24,768]{2,1,0:T(8,128)(2,1)S(1)}, u32[]{:S(2)}, u32[]{:S(2)}) async-start(bf16[4,24,768]{2,1,0:T(8,128)(2,1)} %bitcast.29), calls=%async_computation.11 | async-start | bytes 294912 | tf_op jit(solution)/shard_map/all_to_all | solution.py:530
  303.4 4.4 %all-to-all-done.10 = bf16[4,24,768]{2,1,0:T(8,128)(2,1)S(1)} async-done(((bf16[4,24,768]{2,1,0:T(8,128)(2,1)}), bf16[4,24,768]{2,1,0:T(8,128)(2,1)S(1)}, u32[]{:S(2)}, u32[]{:S(2)}) %all-to-all-start.10) | async-done | bytes 147488 | tf_op jit(solution)/shard_map/all_to_all | solution.py:530
  308.5 3.7 %reduce-scatter.8.cloned.1.call-done = bf16[64,768]{1,0:T(8,128)(2,1)} async-done(((bf16[256,768]{1,0:T(8,128)(2,1)}), bf16[64,768]{1,0:T(8,128)(2,1)}) %reduce-scatter.8.cloned.1.call-update) | async-done | bytes 98320 | tf_op jit(solution)/shard_map/reduce_scatter | solution.py:607
  (61 shorter events, 34.8 us)
Async XLA Ops:
  28.2 20.4 %all-to-all-start = ((bf16[16,8,768]{2,1,0:T(8,128)(2,1)}), bf16[16,8,768]{2,1,0:T(8,128)(2,1)S(1)}, u32[]{:S(2)}, u32[]{:S(2)}) async-start(bf16[16,8,768]{2,1,0:T(8,128)(2,1)} %bitcast.81), calls=%async_computation | async-start | bytes 393216 | tf_op jit(solution)/shard_map/all_to_all | solution.py:530
  36.7 229.0 %reduce-scatter.6.cloned.1.call-start = ((), (), s32[]{:S(2)}) async-start(), calls=%async_computation.15 | async-start | bytes 6684672 | tf_op jit(solution)/shard_map/reduce_scatter | solution.py:606
  48.7 0.7 copy-start.1
  124.6 8.9 %collective-permute-start.2 = (bf16[128,7168]{1,0:T(8,128)(2,1)}, bf16[128,7168]{1,0:T(8,128)(2,1)S(1)}, u32[]{:S(2)}, u32[]{:S(2)}) collective-permute-start(bf16[128,7168]{1,0:T(8,128)(2,1)} %get-tuple-element.62.sent), channel_id=1, source_target_pairs={{0,16},{16,0},{32,48},{48,32},{64,80},{80,64},{96,112},{112,96},{1... | collective-permute-start | bytes 5505032 | tf_op jit(solution)/shard_map/ppermute | solution.py:600
  133.5 1.2 copy-start
  141.4 0.9 copy-start.4
  229.1 29.3 %all-to-all-start.8 = ((bf16[128,8,512]{2,1,0:T(8,128)(2,1)}), bf16[128,8,512]{2,1,0:T(8,128)(2,1)S(1)}, u32[]{:S(2)}, u32[]{:S(2)}) async-start(bf16[128,8,512]{2,1,0:T(8,128)(2,1)} %bitcast.68), calls=%async_computation.8 | async-start | bytes 2097152 | tf_op jit(solution)/shard_map/all_to_all | solution.py:530
  239.7 11.2 %copy-start.2 = (bf16[128,2816]{1,0:T(8,128)(2,1)S(1)}, bf16[128,2816]{1,0:T(8,128)(2,1)}, u32[]{:S(2)}) copy-start(bf16[128,2816]{1,0:T(8,128)(2,1)} %get-tuple-element.60.sent) | copy-start | bytes 2162692
  239.8 42.2 %reduce-scatter.4.cloned.1.call-start = ((), (), s32[]{:S(2)}) async-start(), calls=%async_computation.14 | async-start | bytes 1327104 | tf_op jit(solution)/shard_map/reduce_scatter | solution.py:642
  250.9 3.0 collective-permute-start.1
  253.9 0.9 copy-start.3
  258.4 39.1 %all-to-all-start.9 = ((bf16[16,96,768]{2,1,0:T(8,128)(2,1)}), bf16[16,96,768]{2,1,0:T(8,128)(2,1)S(1)}, u32[]{:S(2)}, u32[]{:S(2)}) async-start(bf16[16,96,768]{2,1,0:T(8,128)(2,1)} %bitcast.66), calls=%async_computation.10 | async-start | bytes 4718592 | tf_op jit(solution)/shard_map/all_to_all | solution.py:530
  264.8 47.5 %reduce-scatter.8.cloned.1.call-start = ((), (), s32[]{:S(2)}) async-start(), calls=%async_computation.16 | async-start | bytes 491520 | tf_op jit(solution)/shard_map/reduce_scatter | solution.py:607
  282.0 20.4 %collective-permute-start = (f32[48,768]{1,0:T(8,128)}, f32[48,768]{1,0:T(8,128)S(1)}, u32[]{:S(2)}, u32[]{:S(2)}) collective-permute-start(f32[48,768]{1,0:T(8,128)} %reduce-scatter.4.cloned.1.call-done), channel_id=1, source_target_pairs={{0,0},{1,8},{2,16},{3,24},{4,32},{5,40},{6,48},{7,56},{8,64},{9,72... | collective-permute-start | bytes 442376 | tf_op jit(solution)/shard_map/ppermute | solution.py:644
  298.5 9.4 %all-to-all-start.10 = ((bf16[4,24,768]{2,1,0:T(8,128)(2,1)}), bf16[4,24,768]{2,1,0:T(8,128)(2,1)S(1)}, u32[]{:S(2)}, u32[]{:S(2)}) async-start(bf16[4,24,768]{2,1,0:T(8,128)(2,1)} %bitcast.29), calls=%async_computation.11 | async-start | bytes 294912 | tf_op jit(solution)/shard_map/all_to_all | solution.py:530
Sparse Core Ops, SparseCore 0:
  141.6 84.8 reduce-scatter.5
  251.0 30.9 reduce-scatter.3
  284.4 27.8 reduce-scatter.7

commit v2 on v1

v2 whole, which is shorter than its diff:
```python
import functools

import jax
import jax.numpy as jnp
from jax import lax
from jax.experimental import pallas as pl
from jax.experimental.pallas import tpu as pltpu
from jax.sharding import PartitionSpec as P

f32 = jnp.float32
bf16 = jnp.bfloat16
i32 = jnp.int32

norm_eps = 1e-05
head_scale = 0.125
neg_fill = -1e30

D = 768
C_IN = 512
FF = 3072
GROUPS = 16
GW = 48
KW = 128
SUPER = 16
TAP_BLOCKS = 9
ROWS = 128
SEQ = 16
PAIRS = 6
MIB = 1024 * 1024
TRANSPOSE_SCRATCH = pltpu.VMEM((D, 128), f32)

def nn(a, b):
    return lax.dot_general(a, b, (((1,), (0,)), ((), ())), preferred_element_type=f32)


def nt(a, b):
    return lax.dot_general(a, b, (((1,), (1,)), ((), ())), preferred_element_type=f32)


def tn(a, b):
    return lax.dot_general(a, b, (((0,), (0,)), ((), ())), preferred_element_type=f32)


def iota(shape, dim):
    return lax.broadcasted_iota(i32, shape, dim)


def int_div(x, c):
    return ((x.astype(f32) + 0.5) * (1.0 / c)).astype(i32)


def stats(x):
    c = x - jnp.mean(x, axis=-1, keepdims=True)
    r = lax.rsqrt(jnp.mean(c * c, axis=-1, keepdims=True) + norm_eps)
    return c * r, r


def norm_back(xhat, r, gain, g):
    e = g * gain
    dx = r * (e - jnp.mean(e, axis=-1, keepdims=True) - xhat * jnp.mean(e * xhat, axis=-1, keepdims=True))
    return dx, jnp.sum(g * xhat, axis=0, keepdims=True), jnp.sum(g, axis=0, keepdims=True)


def cdf(x):
    return 0.5 * (1.0 + lax.erf(x * 0.7071067811865476))


def gelu(x):
    return x * cdf(x)


def gelu_slope(x):
    return cdf(x) + x * (0.3989422804014327 * jnp.exp(-0.5 * x * x))


def col_sum(x):
    return jnp.sum(x.astype(f32), axis=0, keepdims=True)


def vec(lazy):
    ref = lazy()
    return ref[...].astype(f32).reshape(1, ref.shape[0])


def swap_blocks(xs):
    ys = [pltpu.roll(x, f * GW, 1) if f else x for f, x in enumerate(xs)]
    lane = iota((8, 128), 1)
    outs = []
    for g in range(GROUPS):
        tiles = []
        for v in range(D // 128):
            lo, hi = (128 * v) // GW, (128 * v + 127) // GW
            tile = ys[(lo - g) % 16][:, v * 128 : (v + 1) * 128]
            for q in range(lo + 1, hi + 1):
                tile = jnp.where(lane >= q * GW - 128 * v, ys[(q - g) % 16][:, v * 128 : (v + 1) * 128], tile)
            tiles.append(tile)
        w = jnp.concatenate(tiles, axis=1)
        outs.append(pltpu.roll(w, D - g * GW, 1) if g else w)
    return outs


LANE_TILES = D // 128


def rows_to_groups(x, scratch, out_ref):
    for v in range(LANE_TILES):
        scratch[v * ROWS : (v + 1) * ROWS, :] = x[:, v * 128 : (v + 1) * 128]
    outs = swap_blocks(
        [
            jnp.concatenate([scratch[pl.ds(v * ROWS + f, 8, stride=SUPER), :] for v in range(LANE_TILES)], axis=1)
            for f in range(SUPER)
        ]
    )
    for g in range(0, GROUPS, 2):
        out_ref[g * 8 : g * 8 + 16, :] = jnp.concatenate(outs[g : g + 2], axis=0).astype(out_ref.dtype)


def groups_to_rows(in_ref, scratch):
    xs = [in_ref[g].astype(f32)[:8] for g in range(GROUPS)]
    for f, x in enumerate(swap_blocks(xs)):
        for v in range(LANE_TILES):
            scratch[pl.ds(v * ROWS + f, 8, stride=SUPER), :] = x[:, v * 128 : (v + 1) * 128]
    return jnp.concatenate([scratch[v * ROWS : (v + 1) * ROWS, :] for v in range(LANE_TILES)], axis=1)


class Hbm:
    def __init__(self, array):
        self.array = array


class Raw(Hbm):
    pass


class Smem(Hbm):
    pass


class Spill:
    def __init__(self, dims, dtype, parts=1):
        self.struct, self.parts = jax.ShapeDtypeStruct(dims, dtype), parts


class Flusher:
    def __init__(self, ref, target, sems, base, copies):
        self.ref, self.target, self.sems, self.next, self.copies = ref, target, sems, base, copies

    def put(self, value):
        self.ref[...] = value
        self.flush()

    def flush(self, *index):
        src, dst = (self.ref.at[index], self.target.at[index]) if index else (self.ref, self.target)
        copy = pltpu.make_async_copy(src, dst, self.sems.at[self.next])
        copy.start()
        self.next += 1
        self.copies.append(copy)


class Lazy:
    def __init__(self, copy, ref):
        self.copy, self.ref, self.waited = copy, ref, False

    def __call__(self):
        if not self.waited:
            self.copy.wait()
            self.waited = True
        return self.ref


def call(body, outs, *args, scratch=(), flops=0, name=None, mib=16):
    fetched = [k for k, a in enumerate(args) if type(a) in (Hbm, Smem)]
    spilled = [k for k, o in enumerate(outs) if isinstance(o, Spill)]
    arrays = [
        pltpu.with_memory_space_constraint(a.array, pltpu.HBM) if isinstance(a, Hbm) and not isinstance(a, Smem) else getattr(a,'array',a) for a in args
    ]
    structs = [o.struct if isinstance(o, Spill) else o for o in outs]
    near = {Hbm: pltpu.VMEM, Smem: pltpu.SMEM}
    own = [near[type(args[k])](arrays[k].shape, arrays[k].dtype) for k in fetched]
    own += [pltpu.VMEM(structs[k].shape, structs[k].dtype) for k in spilled]
    sem_count = len(fetched) + sum(outs[k].parts for k in spilled)
    if sem_count:
        own.append(pltpu.SemaphoreType.DMA((sem_count,)))

    def wrapped(*refs):
        n_in, n_out = len(args), len(outs)
        ins, out_refs, rest = list(refs[:n_in]), list(refs[n_in : n_in + n_out]), list(refs[n_in + n_out :])
        extra, rest = rest[: len(own)], rest[len(own) :]
        lazies, flushed = [], []
        for slot, k in enumerate(fetched):
            copy = pltpu.make_async_copy(ins[k], extra[slot], extra[-1].at[slot])
            copy.start()
            ins[k] = Lazy(copy, extra[slot])
            lazies.append(ins[k])
        base = len(fetched)
        for slot, k in enumerate(spilled):
            out_refs[k] = Flusher(extra[len(fetched) + slot], out_refs[k], extra[-1], base, flushed)
            base += outs[k].parts
        body(*ins, *out_refs, *rest)
        for lazy in lazies:
            lazy()
        for copy in flushed:
            copy.wait()

    bytes_accessed = sum(a.size * a.dtype.itemsize for a in arrays) + sum(o.size * o.dtype.itemsize for o in structs)
    return pl.pallas_call(
        wrapped,
        out_shape=[pltpu.HBM(o.struct.shape, o.struct.dtype) if isinstance(o, Spill) else o for o in outs],
        in_specs=[pl.BlockSpec(memory_space=pltpu.HBM if isinstance(a, Hbm) else pltpu.VMEM) for a in args],
        out_specs=[pl.BlockSpec(memory_space=pltpu.HBM if isinstance(o, Spill) else pltpu.VMEM) for o in outs],
        scratch_shapes=own + list(scratch),
        compiler_params=pltpu.CompilerParams(vmem_limit_bytes=mib * MIB),
        cost_estimate=pl.CostEstimate(flops=flops, bytes_accessed=bytes_accessed, transcendentals=0),
        name=name,
    )(*arrays)


def fetch(sems, *pairs):
    copies = [pltpu.make_async_copy(src, dst, sems.at[k]) for k, (src, dst) in enumerate(pairs)]
    for copy in copies:
        copy.start()
    return copies


def shape(dims, dtype):
    return jax.ShapeDtypeStruct(dims, dtype)


def live_rows(lengths):
    row = iota((ROWS, 1), 0)
    frame = (row & 63) + lax.axis_index("seq") * 64
    ref = lengths()
    length = jnp.where(row < 64, ref[0], ref[1])
    return (frame < length).astype(f32)


def head_utterance():
    return (lax.axis_index("seq") >= PAIRS).astype(i32)


def core_index():
    return lax.axis_index("batch") & 1


def project_kernel(lengths, feats, gain, shift, weight, bias, masked_out, send_out, scratch):
    xhat, _ = stats(feats()[...].astype(f32))
    normed = (xhat * vec(gain) + vec(shift)).astype(bf16)
    masked = (nn(normed, weight()[...]) + vec(bias)) * live_rows(lengths)
    masked_out.put(masked)
    rows_to_groups(masked, scratch, send_out)


def make_band(taps, out):
    flat = jnp.concatenate([taps[...].astype(f32), jnp.zeros((GW, D), f32)], axis=1)
    for f in range(SUPER):
        rolled = pltpu.roll(flat, f * GW, 1) if f else flat
        out[f * GW : (f + 1) * GW, :] = rolled.astype(bf16)


def shift_matrix(delta):
    r, c = iota((ROWS, ROWS), 0), iota((ROWS, ROWS), 1)
    frame_r = (r >> 3) * 4 + (r & 3)
    frame_c = (c >> 3) * 4 + (c & 3)
    return ((frame_c == frame_r + delta) & ((r & 4) == (c & 4))).astype(f32).astype(bf16)


def conv_kernel(x_in, taps, out, w):
    make_band(taps(), w)
    x = x_in()[...]
    windows = [nn(shift_matrix(i - 4), x).astype(bf16) for i in range(TAP_BLOCKS)]
    out[...] = nt(jnp.concatenate(windows, axis=1), w[...]).astype(out.dtype)


QKV_ROWS = 32
CHUNK = 40
Y_OUTER, Y_OUTPUT, Y_END = 96, 192, 224
HOP = 80


def conv_gradient(got):
    pieces = [got[g, QKV_ROWS:CHUNK, :].astype(f32) for g in range(GROUPS)]
    return jnp.concatenate(pieces, axis=0).astype(bf16)


def conv_back_kernel(got_in, taps, out, w):
    make_band(taps(), w)
    grad = conv_gradient(got_in())
    total = jnp.zeros((ROWS, D), f32)
    for i in range(TAP_BLOCKS):
        total += nn(nn(shift_matrix(4 - i), grad).astype(bf16), w[:, i * D : (i + 1) * D])
    out[...] = total.astype(bf16)


def conv_weight_kernel(got_in, other_in, x_in, x_other, out, *rest):
    tap_outs, (wide, acc, spread, chunks) = rest[:4], rest[4:]
    core = core_index()
    src, dst = iota((D, 384), 0), iota((D, 384), 1)
    f = int_div(dst, 24)
    y = int_div(dst - 24 * f, 6)
    own_taps = (src == f * GW + (2 * y + core) * 6 + (dst - 24 * f - 6 * y)).astype(f32).astype(bf16)
    grads, windows = [], []
    for ref, values in ((got_in(), x_in()), (other_in(), x_other())):
        grads.append(nn(conv_gradient(ref), own_taps).astype(bf16))
        x = values[...]
        windows.append(
            jnp.concatenate([nn(shift_matrix(i - 4), x).astype(bf16) for i in range(TAP_BLOCKS)], axis=1)
        )
    width = TAP_BLOCKS * D
    wide[...] = tn(jnp.concatenate(grads, axis=0), jnp.concatenate(windows, axis=0))
    acc[:, width - 384 :] = jnp.zeros((24, 384), f32)
    for f in range(7, -1, -1):
        acc[:, : width - 384] = (
            (pltpu.roll(acc[...], width - GW, 1)[:, : width - 384] if f < 7 else 0.0)
            + wide[f * 24 : f * 24 + 24, : width - 384]
            + wide[(f + 8) * 24 : (f + 8) * 24 + 24, 384:]
        )
    for v in range(LANE_TILES):
        lanes = slice(v * 128, (v + 1) * 128)
        for i in range(8):
            spread[pl.ds(i, 24, stride=8), :] = acc[:, i * D + v * 128 : i * D + (v + 1) * 128]
        for y in range(4):
            chunks[y, :, lanes] = spread[y * GW : (y + 1) * GW, :].astype(bf16)
    own_y = lax.axis_index("batch") >> 1
    for k, tap_out in enumerate(tap_outs):
        tap_out.put(chunks[(own_y + k) & 3])
    pairs = []
    for p in range(PAIRS):
        terms = [ref[n, :QKV_ROWS, :].astype(f32) for ref in (got_in(), other_in()) for n in (p, PAIRS + p)]
        pairs.append(terms[0] + terms[1] + terms[2] + terms[3])

    def chunk(x, b, k):
        rows = slice((b & 3) * 8, (b & 3) * 8 + 8)
        start = (b >> 2) * 384 + k * 128
        return x[rows, start : start + 128]

    for y in range(4):
        parts = [
            jnp.concatenate(
                [jnp.where(core == 0, chunk(x, 2 * y, k), chunk(x, 2 * y + 1, k)) for x in pairs], axis=1
            )
            for k in range(3)
        ]
        out[y] = jnp.concatenate(parts, axis=0).astype(bf16)


def conv_sum_kernel(*refs):
    total = refs[0]()[...].astype(f32)
    for ref in refs[1:-1]:
        total += ref()[...].astype(f32)
    refs[-1][...] = total


def hop_kernel(chunks_in, dense_in, spill):
    chunks = chunks_in()
    dense = dense_in()[...]
    dst, src = iota((ROWS, Y_END), 0), iota((ROWS, Y_END), 1)
    y, t = dst >> 5, dst & 31
    q = int_div(t, 6)
    row = q * 24 + y * 6 + (t - 6 * q) + jnp.where(q == 4, 96, 0)
    sixes = nn(((src == row) & (t < 30)).astype(f32).astype(bf16), dense)
    outer = dense[Y_OUTER:Y_OUTPUT].astype(f32)
    for y in range(4):
        pieces = [chunks[y].astype(f32), sixes[y * 32 : y * 32 + 32], outer[y * 24 : y * 24 + 24]]
        spill.ref[y * HOP : (y + 1) * HOP, :] = jnp.concatenate(pieces, axis=0).astype(bf16)
    spill.flush()


def hop_sum_kernel(total_in, qkv_out, inner_out, outer_out, output_out):
    total = total_in()[...].astype(f32)
    for k in range(3):
        qkv_out[:, k * D : (k + 1) * D] = total[8 * k : 8 * k + 6]
    dense = total[24:]
    for q in range(4):
        inner_out[:, q * D : (q + 1) * D] = dense[q * 6 : q * 6 + 6]
    output_out[...] = dense[24:30]
    outer_out[...] = dense[32:]


def hidden_order():
    src, dst = iota((D, 1024), 0), iota((D, 1024), 1)
    j = dst & 7
    col = ((dst >> 3) & 7) * 96 + (dst >> 6) * 6 + j
    return ((src == col) & (j < 6)).astype(f32).astype(bf16)


def qkv_kernel(
    conv, masked, conv_bias, gain, shift, weight, query_bias, value_bias,
    pre_out, hidden_out, send_out, order_out, scratch,
):
    pre = groups_to_rows(conv, scratch) + vec(conv_bias)
    pre_out.put(pre)
    xhat, _ = stats(masked()[...] + gelu(pre))
    hidden = xhat * vec(gain) + vec(shift)
    hidden_out.put(hidden)
    hidden_b = hidden.astype(bf16)
    order_out.put(nn(hidden_b, hidden_order()).astype(bf16))
    zero = jnp.zeros((1, D), f32)
    send = send_out.ref
    for slot, (block, bias) in enumerate(((1, zero), (2, vec(value_bias)), (0, vec(query_bias)))):
        part = (nn(hidden_b, weight()[:, block * D : (block + 1) * D]) + bias).astype(bf16)
        for u in range(2):
            for pair in range(PAIRS):
                send[u * PAIRS + pair, slot * 64 : (slot + 1) * 64, :] = part[
                    u * 64 : (u + 1) * 64, pair * 128 : (pair + 1) * 128
                ]
    send[2 * PAIRS :] = jnp.zeros((SEQ - 2 * PAIRS, 192, 128), bf16)
    send_out.flush()


Q_BLOCK = 256


def key_mask(lengths):
    ref = lengths()
    length = jnp.where(head_utterance() == 0, ref[0], ref[1])
    return iota((Q_BLOCK, 1024), 1) < length


def attend_kernel(lengths, qkv_in, out, log_spill):
    qkv, log_out = qkv_in(), log_spill.ref
    keys = qkv[:, 0:64, :].reshape(1024, 128)
    values = qkv[:, 64:128, :].reshape(1024, 128)
    left = iota((Q_BLOCK, 128), 1) < 64
    key_live = key_mask(lengths)
    per = Q_BLOCK // 64

    def step(n, carry):
        query = qkv[pl.ds(n * per, per), 128:192, :].reshape(Q_BLOCK, 128) * head_scale
        parts, logs = [], []
        for head in range(2):
            own = left if head == 0 else ~left
            scores = nt(jnp.where(own, query, jnp.zeros_like(query)), keys)
            scores = jnp.where(key_live, scores, neg_fill)
            top = jnp.max(scores, axis=-1, keepdims=True)
            e = jnp.exp(scores - top)
            total = jnp.sum(e, axis=-1, keepdims=True)
            parts.append(nn(e.astype(bf16), values) * (1.0 / total))
            logs.append(top + jnp.log(total))
        rows = pl.ds(pl.multiple_of(n * Q_BLOCK, Q_BLOCK), Q_BLOCK)
        out[rows, :] = jnp.where(left, parts[0], parts[1]).astype(bf16)
        log_out[rows, :] = jnp.where(left, logs[0], logs[1])
        return carry

    lax.fori_loop(0, 1024 // Q_BLOCK, step, 0)
    log_spill.flush()


def attend_back_kernel(lengths, qkv_in, grad, logs_in, spill, dk, dv):
    qkv, logs, out = qkv_in(), logs_in(), spill.ref
    keys = qkv[:, 0:64, :].reshape(1024, 128)
    values = qkv[:, 64:128, :].reshape(1024, 128)
    left = iota((Q_BLOCK, 128), 1) < 64
    key_live = key_mask(lengths)
    per = Q_BLOCK // 64
    dk[...] = jnp.zeros_like(dk)
    dv[...] = jnp.zeros_like(dv)

    def step(n, carry):
        query = qkv[pl.ds(n * per, per), 128:192, :].reshape(Q_BLOCK, 128) * head_scale
        rows = pl.ds(pl.multiple_of(n * Q_BLOCK, Q_BLOCK), Q_BLOCK)
        go = grad[rows, :]
        parts = []
        for head in range(2):
            own = left if head == 0 else ~left
            q_h = jnp.where(own, query, jnp.zeros_like(query))
            g_h = jnp.where(own, go, jnp.zeros_like(go))
            scores = jnp.where(key_live, nt(q_h, keys), neg_fill)
            probs = jnp.exp(scores - logs[rows, head * 64 : head * 64 + 1])
            grad_probs = nt(g_h, values)
            delta = jnp.sum(probs * grad_probs, axis=-1, keepdims=True)
            grad_scores = (probs * (grad_probs - delta)).astype(bf16)
            parts.append(nn(grad_scores, keys))
            dk[...] += tn(grad_scores, q_h)
            dv[...] += tn(probs.astype(bf16), g_h)
        grad_query = (jnp.where(left, parts[0], parts[1]) * head_scale).astype(bf16)
        out[pl.ds(n * per, per), 0:64, :] = grad_query.reshape(per, 64, 128)
        return carry

    lax.fori_loop(0, 1024 // Q_BLOCK, step, 0)
    out[:, 64:128, :] = dk[...].astype(bf16).reshape(SEQ, 64, 128)
    out[:, 128:192, :] = dv[...].astype(bf16).reshape(SEQ, 64, 128)
    spill.flush()


def head_grads_kernel(hidden_in, grads_in, spill):
    hidden, grads, out = hidden_in(), grads_in(), spill.ref
    rows = hidden[:, head_utterance()].reshape(1024, 1024)
    right = jnp.concatenate([grads[:, k * 64 : (k + 1) * 64, :].reshape(1024, 128) for k in range(3)], axis=1)
    res = tn(rows, right)
    for s in range(SEQ):
        for half in range(2):
            out[s * 32 : s * 32 + 32, half * 384 : half * 384 + 384] = res[
                s * 64 + half * 32 : s * 64 + half * 32 + 32
            ].astype(bf16)
    spill.flush()


def owner_order(core):
    src, dst = iota((D, D), 0), iota((D, D), 1)
    second = dst >= 384
    rest = dst - jnp.where(second, 384, 0)
    which = jnp.where(second, 1 - core, core)
    s = int_div(rest, 24)
    y = int_div(rest - 24 * s, 6)
    j = rest - 24 * s - 6 * y
    return (src == (2 * y + which) * 96 + s * 6 + j).astype(f32).astype(bf16)


S_MID, S_GI, S_INNER, S_GO, S_ATT, S_GA, S_END = 0, 384, 3456, 4992, 5760, 6144, 6912
O_MID, O_INNER, O_ATT, O_END = 0, 384, 1920, 2304


def middle_kernel(
    skip, recv, hidden, cot, out_w_in, out_b, mid_g_in, mid_s_in, inner_w_in, inner_b_in, outer_w_in, outer_b,
    fin_g_in, fin_s_in,
    act_out, grad_att_out, gmi_out, send_out, own_out, small_out,
    act, slope, out_w, inner_w, outer_w, sems,
):
    pairs = [(out_w_in, out_w)]
    for q in range(4):
        cols = slice(q * D, (q + 1) * D)
        pairs += [(inner_w_in.at[:, cols], inner_w.at[:, cols]), (outer_w_in.at[cols, :], outer_w.at[cols, :])]
    copies = fetch(sems, *pairs)
    core = core_index()
    keep = (1 - skip()[0]).astype(f32)
    mid_gain, fin_gain, inner_bias = vec(mid_g_in), vec(fin_g_in), vec(inner_b_in)
    att = jnp.concatenate(
        [jnp.concatenate([recv[u * PAIRS + p] for p in range(PAIRS)], axis=1) for u in range(2)], axis=0
    )
    copies[0].wait()
    middle_in = hidden()[...] + nn(att, out_w[...]) + vec(out_b)
    xm, rm = stats(middle_in)
    middle = xm * mid_gain + vec(mid_s_in)
    middle_b = middle.astype(bf16)
    order = owner_order(core)
    mid = nn(middle_b, order).astype(bf16)
    att_p = nn(att, order).astype(bf16)
    own, send = own_out, send_out

    own[:, O_MID : O_MID + 384] = mid[:, :384]
    own[:, O_ATT : O_ATT + 384] = att_p[:, :384]
    send[:, S_MID : S_MID + 384] = mid[:, 384:]
    send[:, S_ATT : S_ATT + 384] = att_p[:, 384:]
    outer = jnp.zeros((ROWS, D), f32)
    for q in range(4):
        cols = slice(q * D, (q + 1) * D)
        copies[1 + 2 * q].wait()
        pre = nn(middle_b, inner_w[:, cols]) + inner_bias[:, cols]
        c = cdf(pre)
        inner_b = (pre * c).astype(bf16)
        act[:, cols] = inner_b
        slope[:, cols] = c + pre * (0.3989422804014327 * jnp.exp(-0.5 * pre * pre))
        copies[2 + 2 * q].wait()
        outer += nn(inner_b, outer_w[cols, :])
    first = core == 0
    for y in range(4):
        even = act[:, 2 * y * 384 : (2 * y + 1) * 384]
        odd = act[:, (2 * y + 1) * 384 : (2 * y + 2) * 384]
        own[:, O_INNER + y * 384 : O_INNER + (y + 1) * 384] = jnp.where(first, even, odd)
        send[:, S_INNER + y * 384 : S_INNER + (y + 1) * 384] = jnp.where(first, odd, even)
    final_in = middle + keep * (outer + vec(outer_b))
    xf, rf = stats(final_in)
    act_out.put((xf * fin_gain + vec(fin_s_in)).astype(bf16))
    gfi, fin_g, fin_s = norm_back(xf, rf, fin_gain, cot()[...].astype(f32))
    grad_outer = (keep * gfi).astype(bf16)
    send[:, S_GO : S_GO + D] = grad_outer
    grad_middle = gfi
    for q in range(4):
        cols = slice(q * D, (q + 1) * D)
        grad_inner = (slope[:, cols] * nt(grad_outer, outer_w[cols, :])).astype(bf16)
        send[:, S_GI + q * D : S_GI + (q + 1) * D] = grad_inner
        small_out.ref[3 + q : 4 + q, :] = col_sum(grad_inner)
        grad_middle += nt(grad_inner, inner_w[:, cols])
    gmi, mid_g, mid_s = norm_back(xm, rm, mid_gain, grad_middle)
    gmi_out.put(gmi)
    grad_attn = gmi.astype(bf16)
    send[:, S_GA : S_GA + D] = grad_attn
    grad_att = nt(grad_attn, out_w[...]).astype(bf16)
    for u in range(2):
        for p in range(PAIRS):
            grad_att_out.ref[u * PAIRS + p] = grad_att[u * 64 : (u + 1) * 64, p * 128 : (p + 1) * 128]
    grad_att_out.ref[2 * PAIRS :] = jnp.zeros((SEQ - 2 * PAIRS, 64, 128), bf16)
    grad_att_out.flush()
    for row, value in ((0, fin_g), (1, fin_s), (2, col_sum(grad_outer)), (7, mid_g), (8, mid_s), (9, col_sum(grad_attn))):
        small_out.ref[row : row + 1, :] = value
    small_out.ref[10:16, :] = jnp.zeros((6, D), f32)
    small_out.flush()


def dense_grads_kernel(own, sent, got, spill):
    out = spill.ref

    def right(start):
        return jnp.concatenate([sent[:, start : start + D], got[:, start : start + D]], axis=0)

    def left(start, theirs, width):
        return jnp.concatenate([own[:, start : start + width], got[:, theirs : theirs + width]], axis=0)

    outer = tn(left(O_INNER, S_INNER, 1536), right(S_GO))
    for s in range(SEQ):
        rows = [outer[y * 384 + s * 24 : y * 384 + s * 24 + 24] for y in range(4)]
        out[s, Y_OUTER:Y_OUTPUT, :] = jnp.concatenate(rows, axis=0).astype(bf16)
    spill.flush(slice(None), slice(Y_OUTER, Y_OUTPUT))
    mid = left(O_MID, S_MID, 384)
    for half in range(2):
        res = [tn(mid, right(S_GI + (2 * half + k) * D)) for k in range(2)]
        for s in range(SEQ):
            rows = jnp.concatenate([r[s * 24 : s * 24 + 24] for r in res], axis=0)
            out[s, half * 48 : half * 48 + 48, :] = rows.astype(bf16)
        spill.flush(slice(None), slice(half * 48, half * 48 + 48))
    output = tn(left(O_ATT, S_ATT, 384), right(S_GA))
    for s in range(SEQ):
        rows = jnp.concatenate([output[s * 24 : s * 24 + 24], jnp.zeros((8, D), f32)], axis=0)
        out[s, Y_OUTPUT:, :] = rows.astype(bf16)
    spill.flush(slice(None), slice(Y_OUTPUT, Y_END))


def qkv_back_kernel(
    recv, gmi, pre_in, masked, gain_in, weight, qkv_sums, summed_out, send_out, small_out, scratch, conv_out
):
    pre = pre_in()[...]
    gain = vec(gain_in)
    xhat, r = stats(masked()[...] + gelu(pre))
    grad_hidden = gmi()[...]
    sums = []
    for slot in range(3):
        part = jnp.concatenate(
            [
                jnp.concatenate([recv[u * PAIRS + p, slot * 64 : (slot + 1) * 64, :] for p in range(PAIRS)], axis=1)
                for u in range(2)
            ],
            axis=0,
        )
        sums.append(col_sum(part))
        grad_hidden += nt(part, weight()[:, slot * D : (slot + 1) * D])
    grad_summed, enc_g, enc_s = norm_back(xhat, r, gain, grad_hidden)
    summed_out.put(grad_summed)
    grad_conv = (gelu_slope(pre) * grad_summed).astype(bf16).astype(f32)
    rows_to_groups(grad_conv, scratch, conv_out)
    for g in range(GROUPS):
        send_out[g, :QKV_ROWS, :] = qkv_sums()[g * QKV_ROWS : (g + 1) * QKV_ROWS, :]
        send_out[g, QKV_ROWS:, :] = conv_out[g * 8 : g * 8 + 8, :].astype(bf16)
    for row, value in enumerate((enc_g, enc_s, sums[0], sums[2], jnp.sum(grad_conv, axis=0, keepdims=True))):
        small_out.ref[row : row + 1, :] = value
    small_out.ref[5:8, :] = jnp.zeros((3, D), f32)
    small_out.flush()


def feats_back_kernel(
    lengths, conv, summed, feats, gain_in, shift, weight, small_a, small_b, feats_out, tail_out, rows, spread
):
    xhat, r = stats(feats()[...].astype(f32))
    gain = vec(gain_in)
    normed = (xhat * gain + vec(shift)).astype(bf16)
    grad_proj = ((summed()[...] + groups_to_rows(conv, rows)) * live_rows(lengths)).astype(bf16)
    grad_feats, in_g, in_s = norm_back(xhat, r, gain, nt(grad_proj, weight()[...]))
    feats_out.put(grad_feats)
    proj = tn(normed, grad_proj)
    upper = iota((8, 384), 0) < 4
    for n in range(0, 128, 2):
        a, b = proj[n * 4 : n * 4 + 8, :384], proj[n * 4 : n * 4 + 8, 384:]
        both = jnp.concatenate(
            [jnp.where(upper, a, pltpu.roll(b, 4, 0)), jnp.where(upper, pltpu.roll(a, 4, 0), b)], axis=0
        )
        tail_out[n * 8 : n * 8 + 16, :384] = both.astype(bf16)
    a = lambda k: small_a()[k : k + 1, :]
    b = lambda k: small_b()[k : k + 1, :]
    vectors = [col_sum(grad_proj), b(4), b(0), b(1), b(2), b(3), a(9), a(7), a(8), a(2), a(0), a(1)]
    lane = iota((8, D), 1)
    sub = iota((8, D), 0)
    slot6 = lane - 6 * int_div(lane, 6)
    main = jnp.concatenate([jnp.where(slot6 == sub, v, 0.0) for v in vectors] + [jnp.zeros((32, D), f32)], axis=0)
    lane24, sub24 = iota((24, D), 1), iota((24, D), 0)
    slot24 = lane24 - 24 * int_div(lane24, 24)
    inner = [
        jnp.concatenate(
            [jnp.zeros((96, D), f32), jnp.where(slot24 == sub24, a(3 + k), 0.0), jnp.zeros((8, D), f32)], axis=0
        )
        for k in range(4)
    ]
    lane4, sub4 = iota((8, C_IN), 1) & 3, iota((8, C_IN), 0)
    last = jnp.concatenate(
        [
            jnp.zeros((120, C_IN), f32),
            jnp.where(lane4 == sub4, in_g, 0.0) + jnp.where(lane4 == sub4 - 4, in_s, 0.0),
        ],
        axis=0,
    )
    own = iota((128, D), 0)
    col = iota((128, D), 1)
    pick6 = (int_div(col, 6) == own).astype(f32).astype(bf16)
    pick24 = [(int_div(col, 24) + 32 * k == own).astype(f32).astype(bf16) for k in range(4)]
    pick4 = ((iota((128, C_IN), 1) >> 2) == iota((128, C_IN), 0)).astype(f32).astype(bf16)
    spread[...] = jnp.zeros_like(spread)
    terms = [(pick6, main)] + list(zip(pick24, inner)) + [(pick4, last)]
    high = [(p, m.astype(bf16)) for p, m in terms]
    low = [(p, (m - h.astype(f32)).astype(bf16)) for (p, m), (_, h) in zip(terms, high)]
    for k, part in enumerate((high, low)):
        spread[pl.ds(k, 128, stride=8), :] = functools.reduce(lambda x, y: x + y, [nt(p, m) for p, m in part])
    tail_out[:, 384:] = spread[...].astype(bf16)


def tail_sum_kernel(got_in, proj_out, *vector_outs):
    got = got_in()

    def step(n, total):
        block = got[pl.ds(n * 8, 8)].astype(f32)
        for k in range(8):
            total += block[k]
        return total

    total = lax.fori_loop(0, 16, step, jnp.zeros((8, 512), f32))
    proj_out[:, :384] = total[:4, :384]
    proj_out[:, 384:] = total[4:, :384]
    small = total[0:1, 384:] + total[1:2, 384:]
    starts = [120, 124] + [8 * k for k in range(7)] + [56, 64, 96, 72, 80, 88]
    for start, out in zip(starts, vector_outs):
        out[...] = small[0, start : start + out.shape[0]]


def to_peers(x, axis, groups=None):
    return lax.all_to_all(x, axis, 0, 0, tiled=True, axis_index_groups=groups)


Y_GROUPS = [[0, 2, 4, 6], [1, 3, 5, 7]]


def local(
    feats, lengths, skip_flag, cotangent, input_gain, input_shift, proj_weight, proj_bias, conv_weight, conv_bias,
    encoder_gain, encoder_shift, qkv_weight, query_bias, value_bias, output_weight, output_bias, middle_gain,
    middle_shift, inner_weight, inner_bias, outer_weight, outer_bias, final_gain, final_shift,
):
    seq = lax.axis_index("seq")
    rows_in = feats.reshape(ROWS, C_IN)
    cot = cotangent.reshape(ROWS, D)

    masked, conv_send = call(
        project_kernel,
        [Spill((ROWS, D), f32), shape((ROWS, D), bf16)],
        Smem(lengths), Hbm(rows_in), Hbm(input_gain), Hbm(input_shift), Hbm(proj_weight), Hbm(proj_bias),
        flops=2 * ROWS * C_IN * D, name="project", scratch=[TRANSPOSE_SCRATCH],
    )
    conv_x = to_peers(conv_send, "seq")
    own_taps = lax.dynamic_slice_in_dim(conv_weight, seq * GW, GW, axis=0)
    taps = own_taps.transpose(0, 2, 1).reshape(GW, KW * GW)
    band = pltpu.VMEM((D, TAP_BLOCKS * D), bf16)
    conv_flops = 2 * ROWS * D * D * TAP_BLOCKS
    (conv_y,) = call(
        conv_kernel, [shape((ROWS, D), bf16)], Hbm(conv_x), Hbm(taps), scratch=[band], flops=conv_flops, name="conv", mib=24,
    )
    conv_back = to_peers(conv_y, "seq").reshape(GROUPS, 8, D)
    conv_pre, hidden, qkv_send, hidden_send = call(
        qkv_kernel,
        [
            Spill((ROWS, D), f32), Spill((ROWS, D), f32), Spill((SEQ, 192, 128), bf16), Spill((ROWS, 1024), bf16),
        ],
        conv_back, Hbm(masked), Hbm(conv_bias), Hbm(encoder_gain), Hbm(encoder_shift), Hbm(qkv_weight), Hbm(query_bias),
        Hbm(value_bias), flops=2 * ROWS * D * (3 * D + 1024), name="qkv", scratch=[TRANSPOSE_SCRATCH],
    )
    qkv = to_peers(qkv_send, "seq")
    hidden_all = lax.all_gather(hidden_send, "seq", axis=0, tiled=True).reshape(SEQ, 2, 64, 1024)
    attended, logs = call(
        attend_kernel, [shape((1024, 128), bf16), Spill((1024, 128), f32)], Smem(lengths), Hbm(qkv),
        flops=8 * 1024 * 1024 * 128, name="attend",
    )
    att_recv = to_peers(attended.reshape(SEQ, 64, 128), "seq")
    activations, grad_att_send, gmi, pair_send, pair_own, small_a = call(
        middle_kernel,
        [
            Spill((ROWS, D), bf16), Spill((SEQ, 64, 128), bf16), Spill((ROWS, D), f32),
            shape((ROWS, S_END), bf16), shape((ROWS, O_END), bf16), Spill((16, D), f32),
        ],
        Smem(skip_flag), att_recv, Hbm(hidden), Hbm(cot), Raw(output_weight), Hbm(output_bias), Hbm(middle_gain),
        Hbm(middle_shift), Raw(inner_weight), Hbm(inner_bias), Raw(outer_weight), Hbm(outer_bias), Hbm(final_gain),
        Hbm(final_shift),
        scratch=[
            pltpu.VMEM((ROWS, FF), bf16), pltpu.VMEM((ROWS, FF), f32), pltpu.VMEM((D, D), bf16),
            pltpu.VMEM((D, FF), bf16), pltpu.VMEM((FF, D), bf16), pltpu.SemaphoreType.DMA((9,)),
        ],
        flops=2 * ROWS * (4 * D * FF + 2 * D * D), name="middle", mib=32,
    )
    swap = [(i, i ^ 1) for i in range(8)]
    pair_got = lax.ppermute(pair_send, "batch", swap)
    grad_att = to_peers(grad_att_send, "seq").reshape(1024, 128)
    (dense,) = call(
        dense_grads_kernel, [Spill((SEQ, Y_END, D), bf16, parts=4)], pair_own, pair_send, pair_got,
        flops=2 * 256 * D * 3456, name="dense_grads", mib=24,
    )
    dense_part = lax.psum_scatter(dense.reshape(SEQ * Y_END, D), "seq", scatter_dimension=0, tiled=True)

    (grad_qkv_send,) = call(
        attend_back_kernel, [Spill((SEQ, 192, 128), bf16)], Smem(lengths), Hbm(qkv), grad_att, Hbm(logs),
        scratch=[pltpu.VMEM((1024, 128), f32)] * 2, flops=20 * 1024 * 1024 * 128, name="attend_back",
    )
    grad_qkv = to_peers(grad_qkv_send, "seq")
    (qkv_sums,) = call(
        head_grads_kernel, [Spill((SEQ * QKV_ROWS, D), bf16)], Hbm(hidden_all), Hbm(grad_qkv_send),
        flops=2 * 1024 * 1024 * 384, name="head_grads", mib=24,
    )
    grad_summed, back_send, small_b = call(
        qkv_back_kernel,
        [Spill((ROWS, D), f32), shape((SEQ, CHUNK, D), bf16), Spill((8, D), f32)],
        grad_qkv, Hbm(gmi), Hbm(conv_pre), Hbm(masked), Hbm(encoder_gain), Hbm(qkv_weight), Hbm(qkv_sums),
        scratch=[TRANSPOSE_SCRATCH, pltpu.VMEM((ROWS, D), f32)], flops=2 * ROWS * D * 3 * D, name="qkv_back",
    )
    back_got = to_peers(back_send, "seq")
    back_other = lax.ppermute(back_got, "batch", swap)
    x_other = lax.ppermute(conv_x, "batch", swap)
    (grad_x,) = call(
        conv_back_kernel, [shape((ROWS, D), bf16)], Hbm(back_got), Hbm(taps), scratch=[band], flops=conv_flops,
        name="conv_back", mib=24,
    )
    grad_x_got = to_peers(grad_x, "seq").reshape(GROUPS, 8, D)
    x_other, _ = lax.optimization_barrier((x_other, grad_x))
    qkv_chunks, *tap_chunks = call(
        conv_weight_kernel, [shape((4, 24, D), bf16)] + [Spill((GW, D), bf16) for _ in range(4)], Hbm(back_got), Hbm(back_other), Hbm(conv_x), Hbm(x_other),
        scratch=[
            pltpu.VMEM((384, TAP_BLOCKS * D), f32), pltpu.VMEM((24, TAP_BLOCKS * D), f32), pltpu.VMEM((192, 128), f32),
            pltpu.VMEM((4, GW, D), bf16),
        ],
        flops=conv_flops, name="conv_grads", mib=32,
    )
    dense_part, grad_x_got = lax.optimization_barrier((dense_part, grad_x_got))
    (hop_send,) = call(hop_kernel, [Spill((4 * HOP, D), bf16)], Hbm(qkv_chunks), Hbm(dense_part), name="hop")
    hop_send, small_b, *tap_chunks = lax.optimization_barrier((hop_send, small_b, *tap_chunks))
    hop_got = lax.psum_scatter(hop_send, "batch", scatter_dimension=0, tiled=True, axis_index_groups=Y_GROUPS)
    grad_qkv_weight, grad_inner_weight, grad_outer_weight, grad_output_weight = call(
        hop_sum_kernel,
        [shape((6, 3 * D), f32), shape((6, FF), f32), shape((24, D), f32), shape((6, D), f32)],
        Hbm(hop_got), name="hop_sum",
    )
    tap_got = []
    for k, piece in enumerate(tap_chunks):
        moves = [
            (b * 16 + g, (g // 2) * 16 + 8 * (g % 2) + 2 * ((b // 2 + k) % 4) + b % 2)
            for b in range(8)
            for g in range(GROUPS)
        ]
        tap_got.append(Hbm(lax.ppermute(piece, ("batch", "seq"), moves)))
    (tap_own,) = call(conv_sum_kernel, [shape((GW, D), f32)], *tap_got, name="conv_sum")
    grad_conv_weight = tap_own.reshape(6, KW, GW).transpose(0, 2, 1)

    grad_feats, tail = call(
        feats_back_kernel,
        [Spill((ROWS, C_IN), f32), shape((1024, 512), bf16)],
        Smem(lengths), grad_x_got, Hbm(grad_summed), Hbm(rows_in), Hbm(input_gain), Hbm(input_shift),
        Hbm(proj_weight), Hbm(small_a), Hbm(small_b),
        scratch=[TRANSPOSE_SCRATCH, pltpu.VMEM((1024, 128), f32)], flops=4 * ROWS * C_IN * D, name="feats_back",
    )
    tail_got = to_peers(tail, ("batch", "seq"))
    widths = [4, 4] + [6] * 9 + [24] + [6] * 3
    (
        grad_proj_weight, g_in_g, g_in_s, g_proj_b, g_conv_b, g_enc_g, g_enc_s, g_q_b, g_v_b, g_out_b, g_mid_g, g_mid_s,
        g_inner_b, g_outer_b, g_fin_g, g_fin_s,
    ) = call(
        tail_sum_kernel, [shape((4, D), f32)] + [shape((w,), f32) for w in widths], Hbm(tail_got.reshape(128, 8, 512)),
        name="tail_sum",
    )
    return (
        activations.reshape(2, 64, D), grad_feats.reshape(2, 64, C_IN), g_in_g, g_in_s, grad_proj_weight, g_proj_b,
        grad_conv_weight, g_conv_b, g_enc_g, g_enc_s, grad_qkv_weight, g_q_b, g_v_b, grad_output_weight, g_out_b,
        g_mid_g, g_mid_s, grad_inner_weight, g_inner_b, grad_outer_weight, g_outer_b, g_fin_g, g_fin_s,
    )


def solution(mesh):
    split = P("batch", "seq", None)
    both = ("batch", "seq")
    placed = (split, P("batch"), P("batch"), split) + (P(),) * 21
    row, matrix = P(both), P(both, None)
    return jax.shard_map(
        local,
        mesh=mesh,
        in_specs=placed,
        out_specs=(
            split, split, row, row, matrix, row, P(both, None, None), row, row, row, matrix, row, row, matrix, row,
            row, row, matrix, row, matrix, row, row, row,
        ),
        check_vma=False,
    )
```

time: 325 us -> 260 us (0.80)
  blocking collectives: 96.4 us -> 59.8 us
  local copies, waits for them, and re-layouts: 31.9 us -> 12.8 us
  starting transfers between devices: 41.9 us -> 60.4 us
  Pallas kernels: 95.9 us -> 79.5 us
  waiting for transfers between devices: 37.7 us -> 30.4 us
  other arithmetic: 3.37 us -> 0 us
    all_to_all x7 -> x4, blocking collectives: 96.4 us -> 59.8 us  [to_peers(): return lax.all_to_all(x, axis, 0, 0, tiled=True, axis_index_groups=groups)]
    pallas_call x13 -> x16, Pallas kernels: 95.9 us -> 79.5 us  [call(): pl.pallas_call(wrapped, out_shape=[pltpu.HBM(o.struct.shape, o.struct.dty...]
    ppermute x2 -> x6, starting transfers between devices: 7.73 us -> 22.8 us  [the longest x4 20.5 us: local(): tap_got.append(Hbm(lax.ppermute(piece, ('batch', 'seq'), moves)))]
    reduce_scatter x3 -> x2, waiting for transfers between devices: 19.5 us -> 5.27 us  [the longest x1 3.82 us: local(): lax.psum_scatter(hop_send, 'batch', scatter_dimension=0, tiled=True, axis...]
    unnamed x27 -> x37, local copies, waits for them, and re-layouts: 16.9 us -> 7.01 us
    all_to_all x4 -> x5, waiting for transfers between devices: 12.8 us -> 19.8 us  [to_peers(): return lax.all_to_all(x, axis, 0, 0, tiled=True, axis_index_groups=groups)]
    slice x7 -> x0, local copies, waits for them, and re-layouts: 5.83 us -> none  [the longest x1 1.41 us: local(): dense_own[32:56]]
    all_to_all x4 -> x5, starting transfers between devices: 28.8 us -> 29.4 us  [to_peers(): return lax.all_to_all(x, axis, 0, 0, tiled=True, axis_index_groups=groups)]
  transfers between devices with their start and end apart: 10 -> 15, of which waited for: 6 -> 7; matrix products, arithmetic and copies ran while one was open for 3% -> 3% of each run, Pallas kernels for 16% -> 22%
where the time goes in v2:
time: 260 us; the launch traced here: 258 us
  Pallas kernels  79.5 us (31%)
  starting transfers between devices  60.4 us (23%)
  blocking collectives  59.8 us (23%)
  waiting for transfers between devices  30.4 us (12%)
  between operations  14.8 us (6%)
  local copies, waits for them, and re-layouts  12.8 us (5%)
    pallas_call x16, Pallas kernels, call(): pl.pallas_call(wrapped, out_shape=[pltpu.HBM(o.struct.shape, o.struct.dty...  79.5 us
    all_to_all x4, blocking collectives, to_peers(): return lax.all_to_all(x, axis, 0, 0, tiled=True, axis_index_groups=groups)  59.8 us
    all_to_all x5, starting transfers between devices, to_peers(): return lax.all_to_all(x, axis, 0, 0, tiled=True, axis_index_groups=groups)  29.4 us
    ppermute x4, starting transfers between devices, local(): tap_got.append(Hbm(lax.ppermute(piece, ('batch', 'seq'), moves)))  20.5 us
    all_to_all x5, waiting for transfers between devices, to_peers(): return lax.all_to_all(x, axis, 0, 0, tiled=True, axis_index_groups=groups)  19.8 us
    ppermute x1, starting transfers between devices, local(): pair_got = lax.ppermute(pair_send, 'batch', swap)  7.95 us
    unnamed x37, local copies, waits for them, and re-layouts  7.01 us
  transfers between devices with their start and end apart: 15, of which 7 were waited for; matrix products, arithmetic and copies ran while one was open for 3% of the time, Pallas kernels for 22%

profile of v2, /device:TPU:1, one launch (start us, length us, event | category | flops | bytes accessed | tf_op | source)
XLA Modules:
  0.0 257.7 jit_solution(6712505243437137685)
XLA Ops:
  7.8 3.2 %project.1 = (f32[128,768]{1,0:T(8,128)}, bf16[128,768]{1,0:T(8,128)(2,1)}) custom-call(s32[2]{0:T(128)S(1)} %copy-done.1, bf16[128,512]{1,0:T(8,128)(2,1)} %bitcast.21, bf16[512]{0:T(512)(128)(2,1)} %refs_4_.9, bf16[512]{0:T(512)(128)(2,1)} %refs_5_.9, bf16[512,768]{1,0:T(8,128)(2,1)} %refs_6_.5, bf16[768]{0:T(1024)(128)(2,1)} %refs_5_.5), custom_call_target="tpu_custom_call" | custom-call | flops 100663296 | bytes 1510920 | tf_op jit(solution)/shard_map/project/pallas_call | solution.py:206
  11.1 8.4 %all-to-all-start = ((bf16[16,8,768]{2,1,0:T(8,128)(2,1)}), bf16[16,8,768]{2,1,0:T(8,128)(2,1)S(1)}, u32[]{:S(2)}, u32[]{:S(2)}) async-start(bf16[16,8,768]{2,1,0:T(8,128)(2,1)} %bitcast.1), calls=%async_computation | async-start | bytes 393216 | tf_op jit(solution)/shard_map/all_to_all | solution.py:722
  21.6 3.6 %reshape.91.refs_1_ = bf16[48,6144]{1,0:T(8,128)(2,1)} reshape(bf16[48,128,48]{2,1,0:T(8,128)(2,1)S(1)} %copy.50) | data formatting | bytes 1179648 | tf_op jit(solution)/shard_map/reshape | solution.py:745
  27.4 6.4 %conv.1 = bf16[128,768]{1,0:T(8,128)(2,1)S(1)} custom-call(bf16[128,768]{1,0:T(8,128)(2,1)} %bitcast.23, bf16[48,6144]{1,0:T(8,128)(2,1)} %reshape.91.refs_1_), custom_call_target="tpu_custom_call" | custom-call | flops 1358954496 | bytes 983040 | tf_op jit(solution)/shard_map/conv/pallas_call | solution.py:206
  33.8 11.9 %all_to_all.63.refs_0_ = bf16[16,8,768]{2,1,0:T(8,128)(2,1)S(1)} all-to-all(bf16[16,8,768]{2,1,0:T(8,128)(2,1)S(1)} %bitcast.17), channel_id=1, replica_groups=mesh['batch'=8,'seq'=16] {'seq'}, dimensions={0} | all-to-all | bytes 393216 | tf_op jit(solution)/shard_map/all_to_all | solution.py:722
  45.6 4.2 %qkv.1 = (f32[128,768]{1,0:T(8,128)}, f32[128,768]{1,0:T(8,128)}, bf16[16,192,128]{2,1,0:T(8,128)(2,1)}, bf16[128,1024]{1,0:T(8,128)(2,1)}) custom-call(bf16[16,8,768]{2,1,0:T(8,128)(2,1)S(1)} %all_to_all.63.refs_0_, f32[128,768]{1,0:T(8,128)} %get-tuple-element.77.refs_1_.refs_3_, bf16[768]{0:T(1024)(128)(2,1)} %refs_2_.3, bf16[768]{0:T(1024)(128)(2,1)} %refs_4_.8, ...), custom_call_target="tpu_custom_call" | custom-call | flops 654311424 | bytes 5971456 | tf_op jit(solution)/shard_map/qkv/pallas_call | solution.py:206
  49.8 15.3 %all_to_all.64.refs_1_ = bf16[16,192,128]{2,1,0:T(8,128)(2,1)} all-to-all(bf16[16,192,128]{2,1,0:T(8,128)(2,1)} %get-tuple-element.78), channel_id=1, replica_groups=mesh['batch'=8,'seq'=16] {'seq'}, dimensions={0} | all-to-all | bytes 1572864 | tf_op jit(solution)/shard_map/all_to_all | solution.py:722
  65.1 7.3 %attend.1 = (bf16[1024,128]{1,0:T(8,128)(2,1)}, f32[1024,128]{1,0:T(8,128)}) custom-call(s32[2]{0:T(128)S(1)} %copy-done.2, bf16[16,192,128]{2,1,0:T(8,128)(2,1)} %all_to_all.64.refs_1_), custom_call_target="tpu_custom_call" | custom-call | flops 1073741824 | bytes 1572872 | tf_op jit(solution)/shard_map/attend/pallas_call | solution.py:206
  72.4 3.9 %all-to-all-start.3 = ((bf16[16,64,128]{2,1,0:T(8,128)(2,1)}), bf16[16,64,128]{2,1,0:T(8,128)(2,1)S(1)}, u32[]{:S(2)}, u32[]{:S(2)}) async-start(bf16[16,64,128]{2,1,0:T(8,128)(2,1)} %bitcast.5), calls=%async_computation.3 | async-start | bytes 524288 | tf_op jit(solution)/shard_map/all_to_all | solution.py:722
  77.1 6.4 %all-to-all-done.3.refs_1_ = bf16[16,64,128]{2,1,0:T(8,128)(2,1)S(1)} async-done(((bf16[16,64,128]{2,1,0:T(8,128)(2,1)}), bf16[16,64,128]{2,1,0:T(8,128)(2,1)S(1)}, u32[]{:S(2)}, u32[]{:S(2)}) %all-to-all-start.3) | async-done | bytes 262176 | tf_op jit(solution)/shard_map/all_to_all | solution.py:722
  83.6 12.3 %middle.1 = (bf16[128,768]{1,0:T(8,128)(2,1)}, bf16[16,64,128]{2,1,0:T(8,128)(2,1)}, f32[128,768]{1,0:T(8,128)}, bf16[128,6912]{1,0:T(8,128)(2,1)S(1)}, bf16[128...) custom-call(s32[1]{0:T(128)S(6)} %copy.52.refs_0_, bf16[16,64,128]{2,1,0:T(8,128)(2,1)S(1)} %all-to-all-done.3.refs_1_, ...), custom_call_target="tpu_custom_call" | custom-call | flops 2717908992 | bytes 14744580 | tf_op jit(solution)/shard_map/middle/pallas_call | solution.py:206
  95.9 8.0 %collective-permute-start = (bf16[128,6912]{1,0:T(8,128)(2,1)S(1)}, bf16[128,6912]{1,0:T(8,128)(2,1)S(1)}, u32[]{:S(2)}, u32[]{:S(2)}) collective-permute-start(bf16[128,6912]{1,0:T(8,128)(2,1)S(1)} %get-tuple-element.83.refs_1_), channel_id=1, source_target_pairs={{0,16},{16,0},{32,48},{48,32},{64,80},{80,64},{96,112},{112,96},{1... | collective-permute-start | bytes 5308424 | tf_op jit(solution)/shard_map/ppermute | solution.py:783
  103.8 3.3 %collective-permute-done.refs_2_ = bf16[128,6912]{1,0:T(8,128)(2,1)S(1)} collective-permute-done((bf16[128,6912]{1,0:T(8,128)(2,1)S(1)}, bf16[128,6912]{1,0:T(8,128)(2,1)S(1)}, u32[]{:S(2)}, u32[]{:S(2)}) %collective-permute-start) | collective-permute-done | bytes 1769504 | tf_op jit(solution)/shard_map/ppermute | solution.py:783
  107.2 3.4 %dense_grads.1 = bf16[16,224,768]{2,1,0:T(8,128)(2,1)} custom-call(bf16[128,2304]{1,0:T(8,128)(2,1)S(1)} %get-tuple-element.82.refs_0_, bf16[128,6912]{1,0:T(8,128)(2,1)S(1)} %get-tuple-element.83.refs_1_, bf16[128,6912]{1,0:T(8,128)(2,1)S(1)} %collective-permute-done.refs_2_), custom_call_target="tpu_custom_call" | custom-call | flops 1358954496 | bytes 9633792 | tf_op jit(solution)/shard_map/dense_grads/pallas_call | solution.py:206
  111.6 11.6 %all_to_all.65 = bf16[16,64,128]{2,1,0:T(8,128)(2,1)S(1)} all-to-all(bf16[16,64,128]{2,1,0:T(8,128)(2,1)S(1)} %copy-done.5), channel_id=1, replica_groups=mesh['batch'=8,'seq'=16] {'seq'}, dimensions={0} | all-to-all | bytes 524288 | tf_op jit(solution)/shard_map/all_to_all | solution.py:722
  123.1 10.7 %attend_back.1.refs_1_ = bf16[16,192,128]{2,1,0:T(8,128)(2,1)} custom-call(s32[2]{0:T(128)S(1)} %copy-done.2, bf16[16,192,128]{2,1,0:T(8,128)(2,1)} %all_to_all.64.refs_1_, bf16[1024,128]{1,0:T(8,128)(2,1)S(1)} %bitcast.16, f32[1024,128]{1,0:T(8,128)} %get-tuple-element.85.refs_3_), custom_call_target="tpu_custom_call" | custom-call | flops 2684354560 | bytes 2359304 | tf_op jit(solution)/shard_map/attend_back/pallas_call | solution.py:206
  133.8 3.9 %all-to-all-start.5 = ((bf16[16,192,128]{2,1,0:T(8,128)(2,1)}), bf16[16,192,128]{2,1,0:T(8,128)(2,1)S(1)}, u32[]{:S(2)}, u32[]{:S(2)}) async-start(bf16[16,192,128]{2,1,0:T(8,128)(2,1)} %attend_back.1.refs_1_), calls=%async_computation.6 | async-start | bytes 1572864 | tf_op jit(solution)/shard_map/all_to_all | solution.py:722
  137.7 4.7 %head_grads.1.refs_6_ = bf16[512,768]{1,0:T(8,128)(2,1)} custom-call(bf16[16,2,64,1024]{3,2,1,0:T(8,128)(2,1)} %bitcast.19, bf16[16,192,128]{2,1,0:T(8,128)(2,1)} %attend_back.1.refs_1_), custom_call_target="tpu_custom_call" | custom-call | flops 805306368 | bytes 5767168 | tf_op jit(solution)/shard_map/head_grads/pallas_call | solution.py:206
  142.4 11.8 %all-to-all-done.5.refs_0_ = bf16[16,192,128]{2,1,0:T(8,128)(2,1)S(1)} async-done(((bf16[16,192,128]{2,1,0:T(8,128)(2,1)}), bf16[16,192,128]{2,1,0:T(8,128)(2,1)S(1)}, u32[]{:S(2)}, u32[]{:S(2)}) %all-to-all-start.5) | async-done | bytes 786464 | tf_op jit(solution)/shard_map/all_to_all | solution.py:722
  154.2 5.0 %qkv_back.1 = (f32[128,768]{1,0:T(8,128)}, bf16[16,40,768]{2,1,0:T(8,128)(2,1)S(1)}, f32[8,768]{1,0:T(8,128)}) custom-call(bf16[16,192,128]{2,1,0:T(8,128)(2,1)S(1)} %all-to-all-done.5.refs_0_, f32[128,768]{1,0:T(8,128)} %get-tuple-element.86.refs_1_, f32[128,768]{1,0:T(8,128)} %get-tuple-element.87.refs_2_, f32[128,768]{1,0:T(8,128)} %get-tuple-element.77.refs_1_.refs_3_, ...), custom_call_target="tpu_custom_call" | custom-call | flops 452984832 | bytes 7693824 | tf_op jit(solution)/shard_map/qkv_back/pallas_call | solution.py:206
  159.3 21.1 %all_to_all.66.refs_0_ = bf16[16,40,768]{2,1,0:T(8,128)(2,1)S(1)} all-to-all(bf16[16,40,768]{2,1,0:T(8,128)(2,1)S(1)} %get-tuple-element.89), channel_id=1, replica_groups=mesh['batch'=8,'seq'=16] {'seq'}, dimensions={0} | all-to-all | bytes 1966080 | tf_op jit(solution)/shard_map/all_to_all | solution.py:722
  180.3 2.2 collective-permute-start.1
  182.6 5.6 %conv_back.1 = bf16[128,768]{1,0:T(8,128)(2,1)} custom-call(bf16[16,40,768]{2,1,0:T(8,128)(2,1)} %copy-done.4, bf16[48,6144]{1,0:T(8,128)(2,1)} %reshape.91.refs_1_), custom_call_target="tpu_custom_call" | custom-call | flops 1358954496 | bytes 1769472 | tf_op jit(solution)/shard_map/conv_back/pallas_call | solution.py:206
  188.2 3.8 %all-to-all-start.7 = ((bf16[16,8,768]{2,1,0:T(8,128)(2,1)}), bf16[16,8,768]{2,1,0:T(8,128)(2,1)S(1)}, u32[]{:S(2)}, u32[]{:S(2)}) async-start(bf16[16,8,768]{2,1,0:T(8,128)(2,1)} %bitcast.11), calls=%async_computation.8 | async-start | bytes 393216 | tf_op jit(solution)/shard_map/all_to_all | solution.py:722
  193.7 5.8 %conv_grads.1 = (bf16[4,24,768]{2,1,0:T(8,128)(2,1)S(1)}, bf16[48,768]{1,0:T(8,128)(2,1)}, bf16[48,768]{1,0:T(8,128)(2,1)}, bf16[48,768]{1,0:T(8,128)(2,1)}, bf16[48,768]{1,0:T(8,128)(2,1)}) custom-call(bf16[16,40,768]{2,1,0:T(8,128)(2,1)} %copy-done.4, bf16[16,40,768]{2,1,0:T(8,128)(2,1)} %copy-done.12, bf16[128,768]{1,0:T(8,128)(2,1)} %bitcast.24, ...), custom_call_target="tpu_custom_call" | custom-call | flops 1358954496 | bytes 2801664 | tf_op jit(solution)/shard_map/conv_grads/pallas_call | solution.py:206
  201.6 2.1 hop.1
  203.7 4.2 %feats_back.1 = (f32[128,512]{1,0:T(8,128)}, bf16[1024,512]{1,0:T(8,128)(2,1)}) custom-call(s32[2]{0:T(128)S(1)} %copy-done.2, bf16[16,8,768]{2,1,0:T(8,128)(2,1)S(1)} %all-to-all-done.7.refs_1_, f32[128,768]{1,0:T(8,128)} %get-tuple-element.91.refs_2_, bf16[128,512]{1,0:T(8,128)(2,1)} %bitcast.22, bf16[512]{0:T(512)(128)(2,1)} %refs_4_.9, ...), custom_call_target="tpu_custom_call" | custom-call | flops 201326592 | bytes 2893832 | tf_op jit(solution)/shard_map/feats_back/pallas_call | solution.py:206
  208.0 9.4 %all-to-all-start.8 = ((bf16[128,8,512]{2,1,0:T(8,128)(2,1)}), bf16[128,8,512]{2,1,0:T(8,128)(2,1)S(1)}, u32[]{:S(2)}, u32[]{:S(2)}) async-start(bf16[128,8,512]{2,1,0:T(8,128)(2,1)} %bitcast.13), calls=%async_computation.9 | async-start | bytes 2097152 | tf_op jit(solution)/shard_map/all_to_all | solution.py:722
  218.1 3.7 %collective-permute-start.3 = (bf16[48,768]{1,0:T(8,128)(2,1)S(1)}, bf16[48,768]{1,0:T(8,128)(2,1)S(1)}, u32[]{:S(2)}, u32[]{:S(2)}) collective-permute-start(bf16[48,768]{1,0:T(8,128)(2,1)S(1)} %copy-done.17), channel_id=1, source_target_pairs={{0,0},{1,8},{2,16},{3,24},{4,32},{5,40},{6,48},{7,56},{8,64},{9,72... | collective-permute-start | bytes 221192 | tf_op jit(solution)/shard_map/ppermute | solution.py:839
  221.8 5.7 %collective-permute-start.4 = (bf16[48,768]{1,0:T(8,128)(2,1)S(1)}, bf16[48,768]{1,0:T(8,128)(2,1)S(1)}, u32[]{:S(2)}, u32[]{:S(2)}) collective-permute-start(bf16[48,768]{1,0:T(8,128)(2,1)S(1)} %copy-done.16), channel_id=1, source_target_pairs={{0,2},{1,10},{2,18},{3,26},{4,34},{5,42},{6,50},{7,58},{8,66},{9,7... | collective-permute-start | bytes 221192 | tf_op jit(solution)/shard_map/ppermute | solution.py:839
  229.6 9.0 %collective-permute-start.6 = (bf16[48,768]{1,0:T(8,128)(2,1)S(1)}, bf16[48,768]{1,0:T(8,128)(2,1)S(1)}, u32[]{:S(2)}, u32[]{:S(2)}) collective-permute-start(bf16[48,768]{1,0:T(8,128)(2,1)S(1)} %copy-done.14), channel_id=1, source_target_pairs={{0,6},{1,14},{2,22},{3,30},{4,38},{5,46},{6,54},{7,62},{8,70},{9,7... | collective-permute-start | bytes 221192 | tf_op jit(solution)/shard_map/ppermute | solution.py:839
  242.7 3.8 %reduce-scatter.5.cloned.1.call-done.refs_0_ = bf16[80,768]{1,0:T(8,128)(2,1)} async-done(((bf16[320,768]{1,0:T(8,128)(2,1)}), bf16[80,768]{1,0:T(8,128)(2,1)}) %reduce-scatter.5.cloned.1.call-update) | async-done | bytes 122896 | tf_op jit(solution)/shard_map/reduce_scatter | solution.py:826
  (62 shorter events, 21.3 us)
Async XLA Ops:
  7.2 0.7 copy-start.1
  11.1 15.6 %all-to-all-start = ((bf16[16,8,768]{2,1,0:T(8,128)(2,1)}), bf16[16,8,768]{2,1,0:T(8,128)(2,1)S(1)}, u32[]{:S(2)}, u32[]{:S(2)}) async-start(bf16[16,8,768]{2,1,0:T(8,128)(2,1)} %bitcast.1), calls=%async_computation | async-start | bytes 393216 | tf_op jit(solution)/shard_map/all_to_all | solution.py:722
  19.5 118.2 %all-gather.2.cloned.1.call-start = ((), (), s32[]{:S(2)}) async-start(), calls=%async_computation.12 | async-start | bytes 4456448 | tf_op jit(solution)/shard_map/all_gather | solution.py:761
  26.7 0.7 copy-start.6
  33.8 31.3 %copy-start.2 = (s32[2]{0:T(128)S(1)}, s32[2]{0:T(128)}, u32[]{:S(2)}) copy-start(s32[2]{0:T(128)} %refs_0_.8) | copy-start | bytes 28
  72.4 11.2 %all-to-all-start.3 = ((bf16[16,64,128]{2,1,0:T(8,128)(2,1)}), bf16[16,64,128]{2,1,0:T(8,128)(2,1)S(1)}, u32[]{:S(2)}, u32[]{:S(2)}) async-start(bf16[16,64,128]{2,1,0:T(8,128)(2,1)} %bitcast.5), calls=%async_computation.3 | async-start | bytes 524288 | tf_op jit(solution)/shard_map/all_to_all | solution.py:722
  76.3 125.4 %reduce-scatter.3.cloned.1.call-start = ((), (), s32[]{:S(2)}) async-start(), calls=%async_computation.11 | async-start | bytes 5849088 | tf_op jit(solution)/shard_map/reduce_scatter | solution.py:789
  95.9 11.3 %collective-permute-start = (bf16[128,6912]{1,0:T(8,128)(2,1)S(1)}, bf16[128,6912]{1,0:T(8,128)(2,1)S(1)}, u32[]{:S(2)}, u32[]{:S(2)}) collective-permute-start(bf16[128,6912]{1,0:T(8,128)(2,1)S(1)} %get-tuple-element.83.refs_1_), channel_id=1, source_target_pairs={{0,16},{16,0},{32,48},{48,32},{64,80},{80,64},{96,112},{112,96},{1... | collective-permute-start | bytes 5308424 | tf_op jit(solution)/shard_map/ppermute | solution.py:783
  110.6 1.0 copy-start.5
  133.8 20.4 %all-to-all-start.5 = ((bf16[16,192,128]{2,1,0:T(8,128)(2,1)}), bf16[16,192,128]{2,1,0:T(8,128)(2,1)S(1)}, u32[]{:S(2)}, u32[]{:S(2)}) async-start(bf16[16,192,128]{2,1,0:T(8,128)(2,1)} %attend_back.1.refs_1_), calls=%async_computation.6 | async-start | bytes 1572864 | tf_op jit(solution)/shard_map/all_to_all | solution.py:722
  142.4 40.1 %copy-start.7 = (bf16[16,8,768]{2,1,0:T(8,128)(2,1)S(1)}, bf16[16,8,768]{2,1,0:T(8,128)(2,1)}, u32[]{:S(2)}) copy-start(bf16[16,8,768]{2,1,0:T(8,128)(2,1)} %copy-done.6) | copy-start | bytes 589828
  180.3 2.3 copy-start.4
  180.3 11.7 %collective-permute-start.1 = (bf16[16,40,768]{2,1,0:T(8,128)(2,1)S(1)}, bf16[16,40,768]{2,1,0:T(8,128)(2,1)S(1)}, u32[]{:S(2)}, u32[]{:S(2)}) collective-permute-start(bf16[16,40,768]{2,1,0:T(8,128)(2,1)S(1)} %all_to_all.66.refs_0_), channel_id=1, source_target_pairs={{0,16},{16,0},{32,48},{48,32},{64,80},{80,64},{96,112},{112,96},{1... | collective-permute-start | bytes 2949128 | tf_op jit(solution)/shard_map/ppermute | solution.py:807
  182.6 9.5 %collective-permute-start.2 = (bf16[128,768]{1,0:T(8,128)(2,1)S(1)}, bf16[128,768]{1,0:T(8,128)(2,1)S(1)}, u32[]{:S(2)}, u32[]{:S(2)}) collective-permute-start(bf16[128,768]{1,0:T(8,128)(2,1)S(1)} %bitcast.25), channel_id=1, source_target_pairs={{0,16},{16,0},{32,48},{48,32},{64,80},{80,64},{96,112},{112,96},{1... | collective-permute-start | bytes 589832 | tf_op jit(solution)/shard_map/ppermute | solution.py:808
  188.2 11.9 %all-to-all-start.7 = ((bf16[16,8,768]{2,1,0:T(8,128)(2,1)}), bf16[16,8,768]{2,1,0:T(8,128)(2,1)S(1)}, u32[]{:S(2)}, u32[]{:S(2)}) async-start(bf16[16,8,768]{2,1,0:T(8,128)(2,1)} %bitcast.11), calls=%async_computation.8 | async-start | bytes 393216 | tf_op jit(solution)/shard_map/all_to_all | solution.py:722
  192.1 0.7 copy-start.13
  192.8 0.9 copy-start.12
  199.5 0.7 copy-start
  200.2 17.9 %copy-start.17 = (bf16[48,768]{1,0:T(8,128)(2,1)S(1)}, bf16[48,768]{1,0:T(8,128)(2,1)}, u32[]{:S(2)}) copy-start(bf16[48,768]{1,0:T(8,128)(2,1)} %get-tuple-element.108) | copy-start | bytes 221188
  200.2 21.6 %copy-start.16 = (bf16[48,768]{1,0:T(8,128)(2,1)S(1)}, bf16[48,768]{1,0:T(8,128)(2,1)}, u32[]{:S(2)}) copy-start(bf16[48,768]{1,0:T(8,128)(2,1)} %get-tuple-element.109) | copy-start | bytes 221188
  200.2 27.3 %copy-start.15 = (bf16[48,768]{1,0:T(8,128)(2,1)S(1)}, bf16[48,768]{1,0:T(8,128)(2,1)}, u32[]{:S(2)}) copy-start(bf16[48,768]{1,0:T(8,128)(2,1)} %get-tuple-element.110) | copy-start | bytes 221188
  200.2 29.4 %copy-start.14 = (bf16[48,768]{1,0:T(8,128)(2,1)S(1)}, bf16[48,768]{1,0:T(8,128)(2,1)}, u32[]{:S(2)}) copy-start(bf16[48,768]{1,0:T(8,128)(2,1)} %get-tuple-element.111) | copy-start | bytes 221188
  208.0 40.1 %all-to-all-start.8 = ((bf16[128,8,512]{2,1,0:T(8,128)(2,1)}), bf16[128,8,512]{2,1,0:T(8,128)(2,1)S(1)}, u32[]{:S(2)}, u32[]{:S(2)}) async-start(bf16[128,8,512]{2,1,0:T(8,128)(2,1)} %bitcast.13), calls=%async_computation.9 | async-start | bytes 2097152 | tf_op jit(solution)/shard_map/all_to_all | solution.py:722
  217.3 29.1 %reduce-scatter.5.cloned.1.call-start = ((), (), s32[]{:S(2)}) async-start(), calls=%async_computation.13 | async-start | bytes 614400 | tf_op jit(solution)/shard_map/reduce_scatter | solution.py:826
  218.1 20.5 %collective-permute-start.3 = (bf16[48,768]{1,0:T(8,128)(2,1)S(1)}, bf16[48,768]{1,0:T(8,128)(2,1)S(1)}, u32[]{:S(2)}, u32[]{:S(2)}) collective-permute-start(bf16[48,768]{1,0:T(8,128)(2,1)S(1)} %copy-done.17), channel_id=1, source_target_pairs={{0,0},{1,8},{2,16},{3,24},{4,32},{5,40},{6,48},{7,56},{8,64},{9,72... | collective-permute-start | bytes 221192 | tf_op jit(solution)/shard_map/ppermute | solution.py:839
  221.8 16.8 %collective-permute-start.4 = (bf16[48,768]{1,0:T(8,128)(2,1)S(1)}, bf16[48,768]{1,0:T(8,128)(2,1)S(1)}, u32[]{:S(2)}, u32[]{:S(2)}) collective-permute-start(bf16[48,768]{1,0:T(8,128)(2,1)S(1)} %copy-done.16), channel_id=1, source_target_pairs={{0,2},{1,10},{2,18},{3,26},{4,34},{5,42},{6,50},{7,58},{8,66},{9,7... | collective-permute-start | bytes 221192 | tf_op jit(solution)/shard_map/ppermute | solution.py:839
  227.5 11.1 %collective-permute-start.5 = (bf16[48,768]{1,0:T(8,128)(2,1)S(1)}, bf16[48,768]{1,0:T(8,128)(2,1)S(1)}, u32[]{:S(2)}, u32[]{:S(2)}) collective-permute-start(bf16[48,768]{1,0:T(8,128)(2,1)S(1)} %copy-done.15), channel_id=1, source_target_pairs={{0,4},{1,12},{2,20},{3,28},{4,36},{5,44},{6,52},{7,60},{8,68},{9,7... | collective-permute-start | bytes 221192 | tf_op jit(solution)/shard_map/ppermute | solution.py:839
  229.6 10.4 %collective-permute-start.6 = (bf16[48,768]{1,0:T(8,128)(2,1)S(1)}, bf16[48,768]{1,0:T(8,128)(2,1)S(1)}, u32[]{:S(2)}, u32[]{:S(2)}) collective-permute-start(bf16[48,768]{1,0:T(8,128)(2,1)S(1)} %copy-done.14), channel_id=1, source_target_pairs={{0,6},{1,14},{2,22},{3,30},{4,38},{5,46},{6,54},{7,62},{8,70},{9,7... | collective-permute-start | bytes 221192 | tf_op jit(solution)/shard_map/ppermute | solution.py:839
  238.6 1.4 copy-start.8
  238.6 1.4 copy-start.9
  238.6 1.3 copy-start.10
  248.1 1.0 copy-start.3
  (1 other events, 0.6 us)
Sparse Core Ops, SparseCore 0:
  50.0 54.8 all-gather.1
  110.8 90.8 reduce-scatter.2
  220.6 25.8 reduce-scatter.4
